TPU v7x, 256 devices: a whole 4x4x8 slice. The times are simulated.
256 devices in a mesh: slab: 64 (over x, z, core), ens: 4 (over y).
Axes of the slice: x: 4, y: 4, z: 8, core: 2. Of those that a mesh axis runs over, the one named last changes fastest.
Arguments:
- field: bfloat16 [4, 64, 32, 128, 128], P('ens', 'slab'), may hold values from -6 to 6
- weight: bfloat16 [1024, 32, 1024], P('slab'), may hold values from -4 to 4
- local_weight: bfloat16 [32, 32], replicated, may hold values from -1 to 1
- bias: float32 [32], replicated, may hold values from -3 to 3
- cotangent: bfloat16 [4, 64, 32, 128, 128], P('ens', 'slab'), may hold values from -6 to 6
Outputs:
- output: bfloat16 [4, 64, 32, 128, 128], P('ens', 'slab')
- grad_field: bfloat16 [4, 64, 32, 128, 128], P('ens', 'slab')
- grad_spectral: float32 [1024, 32, 1024], P('slab')
- grad_local: float32 [32, 32], replicated
- grad_bias: float32 [32], replicated
All inputs are finite; a program needn't handle non-finite values.
Results may differ from a plain program's by a relative error of at most 0.0075.
Values sent between devices are 32-bit elements; how exact they have to be, the bound alone decides.
A program may use at most 128 MiB of HBM per device.

v0:
```python
import math

import jax
import jax.numpy as jnp
from jax import lax
from jax.sharding import PartitionSpec as P


def basis_table(modes, length):
    frequency = jnp.arange(modes, dtype=jnp.int32) - modes // 2
    points = jnp.arange(length, dtype=jnp.int32)
    product = frequency[:, None] * points[None, :] % length
    angles = product.astype(jnp.float32) * (2.0 * math.pi / length)
    return (jnp.cos(angles) + jnp.sin(angles)) / math.sqrt(length)


def local(field, weight, local_weight, bias, cotangent):
    highest = lax.Precision.HIGHEST
    members, planes, channels, cells_x, cells_y = field.shape
    pairs, modes = (weight.shape[0], weight.shape[1])
    depth = planes * lax.axis_size("slab")
    start_plane = lax.axis_index("slab") * planes
    basis_y = basis_table(modes, cells_y)
    basis_round = basis_y.astype(jnp.bfloat16)
    basis_x = basis_table(modes, cells_x)
    basis_z = basis_table(modes, depth)
    basis_local = lax.dynamic_slice_in_dim(basis_z, start_plane, planes, 1)
    mixing = weight.astype(jnp.float32).reshape(pairs, modes, channels, channels)

    def project(data):
        along_y = jnp.einsum(
            "mzcxy,ky->mzcxk", data, basis_round, preferred_element_type=jnp.float32
        )
        along_x = jnp.einsum("mzcxk,jx->mzcjk", along_y, basis_x, precision=highest)
        along_x = along_x.reshape(members, planes, channels, modes * modes)
        partial_modes = jnp.einsum("mzcp,kz->mkcp", along_x, basis_local, precision=highest)
        return lax.psum_scatter(partial_modes, "slab", scatter_dimension=3, tiled=True)

    def synthesize(coefs):
        planes_here = jnp.einsum(
            "mkcp,kz->mzcp",
            lax.all_gather(coefs, "slab", axis=3, tiled=True),
            basis_local,
            precision=highest,
        )
        planes_here = planes_here.reshape(members, planes, channels, modes, modes)
        along_x = jnp.einsum("mzcjk,jx->mzcxk", planes_here, basis_x, precision=highest)
        return jnp.einsum("mzcxk,ky->mzcxy", along_x, basis_y, precision=highest)

    coefs = project(field)
    mixed = jnp.einsum("mkcp,pkco->mkop", coefs, mixing, precision=highest)
    linear = jnp.einsum("mzcxy,co->mzoxy", field, local_weight, preferred_element_type=jnp.float32)
    before = synthesize(mixed) + linear + bias[None, None, :, None, None]
    result, pullback = jax.vjp(jax.nn.gelu, before)
    (slope,) = pullback(cotangent.astype(jnp.float32))
    slope_round = slope.astype(jnp.bfloat16)
    local_part = jnp.einsum(
        "mzcxy,mzoxy->co", field, slope_round, preferred_element_type=jnp.float32
    )
    bias_part = jnp.sum(slope_round.astype(jnp.float32), axis=(0, 1, 3, 4))
    grad_local, grad_bias = lax.psum((local_part, bias_part), ("slab", "ens"))
    back_coefs = project(slope_round)
    mixing_part = jnp.einsum("mkcp,mkop->pkco", coefs, back_coefs, precision=highest)
    grad_mixing = lax.psum(mixing_part, "ens")
    back_modes = jnp.einsum("mkop,pkco->mkcp", back_coefs, mixing, precision=highest)
    pointwise = jnp.einsum(
        "mzoxy,co->mzcxy", slope_round, local_weight, preferred_element_type=jnp.float32
    )
    grad_values = synthesize(back_modes) + pointwise
    return (
        result.astype(jnp.bfloat16),
        grad_values.astype(jnp.bfloat16),
        grad_mixing.reshape(pairs, modes, channels * channels),
        grad_local,
        grad_bias,
    )


def solution(mesh):
    placed = (
        P("ens", "slab", None, None, None),
        P("slab", None, None),
        P(),
        P(),
        P("ens", "slab", None, None, None),
    )
    return jax.shard_map(
        local,
        mesh=mesh,
        in_specs=placed,
        out_specs=(
            P("ens", "slab", None, None, None),
            P("ens", "slab", None, None, None),
            P("slab", None, None),
            P(),
            P(),
        ),
        check_vma=False,
    )
```

profile of v0, /device:TPU:1, one launch (start us, length us, event | category | flops | bytes accessed | tf_op | source)
XLA Modules:
  0.0 718.0 jit_solution(6103786431975974381)
XLA Ops:
  9.0 2.6 convolution_bitcast_fusion.1
  11.9 8.0 %multiply_bitcast_fusion.1 = f32[1,32,32,1024]{2,1,3,0:T(8,128)} fusion(f32[32,1024]{0,1:T(8,128)S(1)} %bitcast.159, f32[32]{0:T(128)S(1)} %bitcast.171), kind=kLoop, calls=%fused_computation.1 | loop fusion | flops 1048576 | bytes 4325504 | tf_op jit(solution)/shard_map/mzcp,kz->mkcp/transpose | solution.py:36
  21.1 4.3 reshape.132
  25.5 183.8 %reduce-scatter.3.cloned.1.call-done = f32[1,32,32,16]{2,1,3,0:T(8,128)} async-done(((f32[1,32,32,1024]{2,1,3,0:T(8,128)}), f32[1,32,32,16]{2,1,3,0:T(8,128)}) %reduce-scatter.3.cloned.1.call-update) | async-done | bytes 65552 | tf_op jit(solution)/shard_map/reduce_scatter | solution.py:37
  209.2 5.7 fusion.2
  216.2 2.1 fusion.23
  218.3 100.0 %all-gather.3.cloned.1.call-done = f32[1,32,32,1024]{2,1,0,3:T(8,128)} async-done(((f32[1,32,32,16]{2,1,0,3:T(8,128)}), f32[1,32,32,1024]{2,1,0,3:T(8,128)}) %all-gather.3.cloned.1.call-update) | async-done | bytes 4194320 | tf_op jit(solution)/shard_map/all_gather | solution.py:42
  318.3 10.7 %fusion.58 = f32[1,32,32,32]{1,0,3,2:T(1,128)S(1)} fusion(f32[32,32,32,32]{0,3,2,1:T(8,128)} %bitcast.156, f32[32,1]{0,1:T(1,128)S(1)} %add_multiply_fusion.7), kind=kOutput, calls=%fused_computation.84 | convolution fusion | flops 12582912 | bytes 4325504 | tf_op jit(solution)/shard_map/mkcp,kz->mzcp/dot_general | solution.py:40
  330.2 8.3 %convert_reduce_fusion = (f32[32]{0:T(128)S(1)}, bf16[1,1,32,128,128]{4,3,2,1,0:T(8,128)(2,1)S(1)}, f32[32,128,128]{2,1,0:T(8,128)}) fusion(bf16[1,1,32,128,128]{4,3,2,1,0:T(8,128)(2,1)S(1)} %copy-done.6, f32[32]{0:T(128)S(1)} %copy-done.7, f32[32,128,128]{2,0,1:T(8,128)} %fusion.23, f32[32,128,32]{1,2,0:T(8,128)S(1)} %bitcast.166, s32[32]{0:T(128)S(1)} %iota_add_fusion), kind=kOutput, calls=%fused_computation.26 | convolution fusion | flops 214499296 | bytes 6816128 | tf_op jit(solution)/shard_map/mzcxk,ky->mzcxy/dot_general | solution.py:48
  339.1 2.6 convolution_bitcast_fusion
  342.0 8.0 %multiply_bitcast_fusion = f32[1,32,32,1024]{2,1,3,0:T(8,128)} fusion(f32[32,1024]{0,1:T(8,128)S(1)} %bitcast.160, f32[32]{0:T(128)S(1)} %bitcast.172), kind=kLoop, calls=%fused_computation | loop fusion | flops 1048576 | bytes 4325504 | tf_op jit(solution)/shard_map/mzcp,kz->mkcp/transpose | solution.py:36
  350.2 181.5 %reduce-scatter.5.cloned.1.call-done = f32[1,32,32,16]{2,1,3,0:T(8,128)} async-done(((f32[1,32,32,1024]{2,1,3,0:T(8,128)}), f32[1,32,32,16]{2,1,3,0:T(8,128)}) %reduce-scatter.5.cloned.1.call-update) | async-done | bytes 65552 | tf_op jit(solution)/shard_map/reduce_scatter | solution.py:37
  531.7 8.9 %fusion = f32[32,16,1,32]{3,2,1,0:T(1,128)S(1)} fusion(bf16[16,32,32,32]{3,2,1,0:T(8,128)(2,1)} %reshape.132, f32[32,32,16,1]{1,0,2,3:T(8,128)} %bitcast.169), kind=kOutput, calls=%fused_computation.3 | convolution fusion | flops 6291456 | bytes 1179648 | tf_op jit(solution)/shard_map/mkop,pkco->mkcp/dot_general | solution.py:65
  541.5 4.5 broadcast_multiply_fusion
  546.0 7.7 %reshape.142 = f32[16,32,1024]{2,1,0:T(8,128)} reshape(f32[16,32,32,32]{3,2,1,0:T(8,128)} %broadcast_multiply_fusion) | data formatting | bytes 4194304 | tf_op jit(solution)/shard_map/reshape | solution.py:73
  555.0 80.8 %all-reduce = (f32[32,32]{0,1:T(8,128)S(1)}, f32[32]{0:T(128)}) all-reduce(f32[32,32]{0,1:T(8,128)S(1)} %convolution_bitcast_fusion.3, f32[32]{0:T(128)S(1)} %get-tuple-element.32), channel_id=1, replica_groups=mesh['slab'=64,'ens'=4] {'slab','ens'}, use_global_device_ids=true, to_apply=%region_3.4 | all-reduce | flops 1056 | bytes 8448 | tf_op jit(solution)/shard_map/psum | solution.py:61
  636.5 2.0 fusion.20
  638.5 3.2 fusion.18
  641.8 3.0 all-gather.5.cloned.1.call-done
  644.7 11.4 %fusion.56 = f32[1,32,32,32]{1,0,3,2:T(1,128)} fusion(f32[32,32,32,32]{0,3,2,1:T(8,128)} %bitcast.155, f32[32,1]{0,1:T(1,128)S(1)} %add_multiply_fusion.7), kind=kOutput, calls=%fused_computation.82 | convolution fusion | flops 12582912 | bytes 4325504 | tf_op jit(solution)/shard_map/mkcp,kz->mzcp/dot_general | solution.py:40
  656.1 2.0 copy.69
  659.8 5.8 fusion.17
  665.6 42.5 %all-reduce.3.cloned.1.call-done = f32[16,32,1024]{2,1,0:T(8,128)} async-done(((f32[16,32,1024]{2,1,0:T(8,128)}), f32[16,32,1024]{2,1,0:T(8,128)}) %all-reduce.3.cloned.1.call-update) | async-done | bytes 2097168 | tf_op jit(solution)/shard_map/psum | solution.py:64
  708.1 3.2 copy.100
  (41 shorter events, 11.6 us)
Async XLA Ops:
  7.2 1.2 copy-start
  7.2 202.1 %reduce-scatter.3.cloned.1.call-start = ((), (), s32[]{:S(2)}) async-start(), calls=%async_computation.2 | async-start | bytes 17039360 | tf_op jit(solution)/shard_map/reduce_scatter | solution.py:37
  19.9 1.2 copy-start.2
  19.9 298.3 %all-gather.3.cloned.1.call-start = ((), (), s32[]{:S(2)}) async-start(), calls=%async_computation.3 | async-start | bytes 17039360 | tf_op jit(solution)/shard_map/all_gather | solution.py:42
  209.2 7.0 copy-start.5
  215.7 316.0 %reduce-scatter.5.cloned.1.call-start = ((), (), s32[]{:S(2)}) async-start(), calls=%async_computation.4 | async-start | bytes 17039360 | tf_op jit(solution)/shard_map/reduce_scatter | solution.py:37
  328.9 1.2 copy-start.6
  328.9 1.2 copy-start.7
  338.5 215.2 %copy-start.1 = (bf16[1,1,32,128,128]{4,3,2,1,0:T(8,128)(2,1)}, bf16[1,1,32,128,128]{4,3,2,1,0:T(8,128)(2,1)S(1)}, u32[]{:S(2)}) copy-start(bf16[1,1,32,128,128]{4,3,2,1,0:T(8,128)(2,1)S(1)} %get-tuple-element.33) | copy-start | bytes 3145732
  350.0 294.7 %all-gather.5.cloned.1.call-start = ((), (), s32[]{:S(2)}) async-start(), calls=%async_computation.5 | async-start | bytes 17039360 | tf_op jit(solution)/shard_map/all_gather | solution.py:42
  531.7 9.8 %copy-start.3 = (f32[1,32,32,16]{2,1,3,0:T(8,128)S(1)}, f32[1,32,32,16]{2,1,3,0:T(8,128)}, u32[]{:S(2)}) copy-start(f32[1,32,32,16]{2,1,3,0:T(8,128)} %reduce-scatter.3.cloned.1.call-done) | copy-start | bytes 196612
  531.7 9.8 %copy-start.4 = (f32[1,32,32,16]{2,1,3,0:T(8,128)S(1)}, f32[1,32,32,16]{2,1,3,0:T(8,128)}, u32[]{:S(2)}) copy-start(f32[1,32,32,16]{2,1,3,0:T(8,128)} %reduce-scatter.5.cloned.1.call-done) | copy-start | bytes 196612
  541.4 166.7 %all-reduce.3.cloned.1.call-start = ((), (), s32[]{:S(2)}) async-start(), calls=%async_computation.6 | async-start | bytes 4194304 | tf_op jit(solution)/shard_map/psum | solution.py:64
Sparse Core Ops, SparseCore 0:
  20.1 189.1 reduce-scatter.2
  215.8 102.3 all-gather.2
  350.1 181.5 reduce-scatter.4
  541.5 103.1 all-gather.4
  647.5 60.5 all-reduce.2
where the time goes:
time: 724 us; the launch traced here: 718 us
  waiting for transfers between devices  511 us (71%)
  blocking collectives  80.8 us (11%)
  matrix products  64.7 us (9%)
  other arithmetic  23.9 us (3%)
  local copies, waits for them, and re-layouts  22.9 us (3%)
  between operations  14.2 us (2%)
    reduce_scatter x2, waiting for transfers between devices, project(): lax.psum_scatter(partial_modes, 'slab', scatter_dimension=3, tiled=True)  365 us
    all_gather x2, waiting for transfers between devices, synthesize(): lax.all_gather(coefs, 'slab', axis=3, tiled=True)  103 us
    psum x1, blocking collectives, local(): grad_local, grad_bias = lax.psum((local_part, bias_part), ('slab', 'ens'))  80.8 us
    psum x1, waiting for transfers between devices, local(): grad_mixing = lax.psum(mixing_part, 'ens')  42.5 us
    dot_general x2, matrix products, synthesize(): jnp.einsum('mkcp,kz->mzcp', lax.all_gather(coefs, 'slab', axis=3, tiled=T...  22 us
    transpose x2, other arithmetic, project(): jnp.einsum('mzcp,kz->mkcp', along_x, basis_local, precision=highest)  16 us
  transfers between devices with their start and end apart: 5, of which 5 were waited for; matrix products, arithmetic and copies ran while one was open for 7% of the time, Pallas kernels for 0%

commit v1 on v0

v1 whole, which is shorter than its diff:
```python
import functools
import math

import jax
import jax.numpy as jnp
import ml_dtypes
import numpy as np
from jax import lax
from jax.experimental import pallas as pl
from jax.experimental.pallas import tpu as pltpu
from jax.sharding import PartitionSpec as P

BF = jnp.bfloat16
F32 = jnp.float32
MESH = pl.DeviceIdType.MESH
C = 32
N = 128
K = 32
NZ = 64
XB = 16
ROOT = math.sqrt(2.0 / math.pi)


def basis_table(modes, length):
    frequency = np.arange(modes, dtype=np.int32) - modes // 2
    points = np.arange(length, dtype=np.int32)
    product = frequency[:, None] * points[None, :] % length
    angles = product.astype(np.float32) * np.float32(2.0 * math.pi / length)
    return (np.cos(angles) + np.sin(angles)) / np.float32(math.sqrt(length))


def split_table(table):
    high = table.astype(ml_dtypes.bfloat16)
    low = (table - high.astype(np.float32)).astype(ml_dtypes.bfloat16)
    return high, low


def three(table):
    high, low = split_table(table)
    return np.concatenate([high, high, low], axis=1)


def tables():
    basis = basis_table(K, N)
    slots = np.arange(NZ)
    basis_z = basis_table(K, NZ)[:, slots % 32 * 2 + slots // 32]
    by16 = basis.astype(ml_dtypes.bfloat16).astype(np.float32)
    wide = np.zeros((2, 8, 16, 8, N), np.float32)
    for c in range(8):
        wide[:, c, :, c, :] = by16.reshape(2, 16, N)
    wide = wide.reshape(256, 8 * N)
    eye8, eye32 = np.eye(8, dtype=np.float32), np.eye(32, dtype=np.float32)
    spread = np.repeat(np.repeat(eye8, 16, axis=0), 32, axis=1)
    to_modes = np.tile(np.repeat(eye32, 16, axis=1), (4, 1))
    from_modes = to_modes.T.reshape(4, 128, 128)
    rows = np.repeat(eye32, XB, axis=0)
    lanes = np.zeros((512, 128), np.float32)
    lanes[:, :32] = rows
    return dict(
        wide_t=wide.T.copy(),
        bx=three(basis),
        wide=wide,
        bz=three(basis_z),
        spread=np.concatenate([spread, spread], axis=0),
        to_modes=np.concatenate([to_modes, to_modes], axis=0),
        bzt=three(basis_z.T),
        bxt=three(basis.T),
        rows=rows,
        rows_t=rows.T.copy(),
        lanes=lanes,
        from_modes=np.concatenate([from_modes, from_modes], axis=1),
        gather=np.concatenate([spread.T, spread.T], axis=0),
    )


TABLES = {name: np.asarray(table).astype(ml_dtypes.bfloat16) for name, table in tables().items()}
NAMES = tuple(TABLES)


def split(value):
    high = value.astype(BF)
    return high, (value - high.astype(F32)).astype(BF)


def dot(a, b):
    return jnp.dot(a, b, preferred_element_type=F32)


def dot_nt(a, b):
    return lax.dot_general(a, b, (((1,), (1,)), ((), ())), preferred_element_type=F32)


def dot_three(table, value):
    high, low = split(value)
    return dot(table, jnp.concatenate([high, low, high], axis=0))


def kernel(n_slab, n_ens, field, weight, lw, bias, cot, *rest):
    consts = dict(zip(NAMES, rest[: len(NAMES)]))
    rest = rest[len(NAMES) :]
    out, gf, gs, gl_out, gb_out = rest[:5]
    rest = rest[5:]
    tab = dict(zip(NAMES, rest[: len(NAMES)]))
    rest = rest[len(NAMES) :]
    (
        field_v, cot_v, w_v, pre, out_v, slope_v, gf_v, gs_v, kl_f, kl_b, s2, cexp, gacc, bsum,
        send, recv, call, ball, glsend, glrecv, glall, glfin_send, glfin,
        load_sem, store_sem, tab_sem, send_sem, recv_sem, ens_send, ens_recv, gl_send, gl_recv,
    ) = rest
    me = lax.axis_index("slab")
    mine = lax.axis_index("ens")

    loads = [
        pltpu.make_async_copy(field, field_v, load_sem.at[0]),
        pltpu.make_async_copy(cot, cot_v, load_sem.at[1]),
        pltpu.make_async_copy(weight, w_v, load_sem.at[2]),
    ]
    tab_loads = {
        name: pltpu.make_async_copy(consts[name], tab[name], tab_sem.at[at])
        for at, name in enumerate(NAMES)
    }
    tab_loads["wide_t"].start()
    loads[0].start()
    for name in NAMES[1:]:
        tab_loads[name].start()
    loads[1].start()
    loads[2].start()

    barrier = pltpu.get_barrier_semaphore()

    def greet(at, carry):
        pl.semaphore_signal(barrier, inc=1, device_id={"slab": lax.rem(me + at, n_slab)}, device_id_type=MESH)
        return carry

    lax.fori_loop(1, n_slab, greet, 0)
    for at in range(1, n_ens):
        pl.semaphore_signal(barrier, inc=1, device_id={"ens": lax.rem(mine + at, n_ens)}, device_id_type=MESH)

    def project(data, phase):
        for g in range(4):
            total = None
            for pair in range(4):
                at = g * 8 + pair * 2
                part = dot(
                    jnp.concatenate([data[at], data[at + 1]], axis=1),
                    tab["wide_t"][pair * 256 : (pair + 1) * 256, :],
                )
                total = part if total is None else total + part
            modes = dot_three(tab["bx"][...], total)
            send[phase, :32, g, :] = modes[:, :128]
            send[phase, 32:, g, :] = modes[:, 128:]

    def exchange(phase):
        def one(at, carry):
            peer = lax.rem(me + at, n_slab)
            pltpu.make_async_remote_copy(
                src_ref=send.at[phase, slot(peer)],
                dst_ref=recv.at[phase, slot(me)],
                send_sem=send_sem.at[phase],
                recv_sem=recv_sem.at[phase],
                device_id={"slab": peer},
                device_id_type=MESH,
            ).start()
            return carry

        lax.fori_loop(1, n_slab, one, 0)
        recv[phase, slot(me)] = send[phase, slot(me)]

    def share(source, target, at_sem):
        for at in range(1, n_ens):
            pltpu.make_async_remote_copy(
                src_ref=source,
                dst_ref=target,
                send_sem=ens_send.at[at_sem],
                recv_sem=ens_recv.at[at_sem],
                device_id={"ens": lax.rem(mine + at, n_ens)},
                device_id_type=MESH,
            ).start()

    def wait_share(ref, at_sem):
        some = ref.at[pl.ds(0, n_ens - 1)]
        pltpu.make_async_copy(some, some, ens_recv.at[at_sem]).wait()

    def wait_share_sent(ref, at_sem):
        some = ref.at[pl.ds(0, n_ens - 1)]
        pltpu.make_async_copy(some, some, ens_send.at[at_sem]).wait()

    def spread_out(source, target, at_sem, row):
        def one(at, carry):
            peer = lax.rem(me + at, n_slab)
            pltpu.make_async_remote_copy(
                src_ref=source.at[peer // 2] if row else source.at[0],
                dst_ref=target.at[slot(me)],
                send_sem=gl_send.at[at_sem],
                recv_sem=gl_recv.at[at_sem],
                device_id={"slab": peer},
                device_id_type=MESH,
            ).start()
            return carry

        lax.fori_loop(1, n_slab, one, 0)

    def owned(phase):
        planes = jnp.concatenate([recv[phase, :, g, :] for g in range(4)], axis=1)
        return dot_three(tab["bz"][...], planes)

    def planes_out(phase, modes):
        planes = dot_three(tab["bzt"][...], modes)
        for g in range(4):
            send[phase, :, g, :] = planes[:, g * 128 : (g + 1) * 128]

    def own_pair(chunk, lanes):
        row = lax.broadcasted_iota(jnp.int32, (128, lanes), 0) // 32 + chunk * 4
        lane = lax.rem(lax.broadcasted_iota(jnp.int32, (128, lanes), 1), 16)
        return row == lane

    def masked(modes, keep):
        tall = jnp.concatenate([modes] * 4, axis=0)
        high, low = split(jnp.where(keep, tall, 0.0))
        return jnp.concatenate([high, low], axis=1)

    def fold(value, keep):
        value = jnp.where(keep, value, 0.0)
        return value[0:32] + value[32:64] + value[64:96] + value[96:128]

    def to_channels(modes, keep):
        total = None
        for g in range(4):
            part = dot(masked(modes[:, g * 128 : (g + 1) * 128], keep), tab["from_modes"][g])
            total = part if total is None else total + part
        return total

    def weights_of(chunk, g):
        return w_v[pl.ds(chunk * 4, 4), :, g * 256 : (g + 1) * 256].reshape(128, 256).astype(F32)

    def narrow(phase):
        for g in range(4):
            modes = jnp.concatenate([recv[phase, :32, g, :], recv[phase, 32:, g, :]], axis=1)
            s2[g] = dot_three(tab["bxt"][...], modes).astype(BF)

    def block_of(ref, at):
        a = ref[:, pl.ds(pl.multiple_of(at * 2 * XB, 2 * XB), XB), :].reshape(C * XB, N)
        b = ref[:, pl.ds(pl.multiple_of(at * 2 * XB + XB, XB), XB), :].reshape(C * XB, N)
        return jnp.concatenate([a, b], axis=1)

    def pointwise(matrix, data):
        def step(at, carry):
            value = dot(matrix[...], block_of(data, at))
            pre[:, pl.ds(pl.multiple_of(at * 2 * XB, 2 * XB), XB), :] = value[:, :N].reshape(C, XB, N)
            pre[:, pl.ds(pl.multiple_of(at * 2 * XB + XB, XB), XB), :] = value[:, N:].reshape(C, XB, N)
            return carry

        lax.fori_loop(0, N // (2 * XB), step, 0)

    tab_loads["wide_t"].wait()
    tab_loads["bx"].wait()
    loads[0].wait()
    project(field_v, 0)
    pl.semaphore_wait(barrier, n_slab - 1 + n_ens - 1)
    exchange(0)

    for name in NAMES[2:]:
        tab_loads[name].wait()
    loads[1].wait()
    loads[2].wait()
    tall = dot(dot_nt(tab["rows"][...], lw[...]).astype(BF), tab["rows_t"][...])
    same = lax.rem(lax.broadcasted_iota(jnp.int32, (512, 512), 0), XB) == lax.rem(
        lax.broadcasted_iota(jnp.int32, (512, 512), 1), XB
    )
    kl_f[...] = jnp.where(same, tall, 0.0).astype(BF)
    tall = dot(dot(tab["rows"][...], lw[...]).astype(BF), tab["rows_t"][...])
    kl_b[...] = jnp.where(same, tall, 0.0).astype(BF)
    pointwise(kl_f, field_v)

    wait_all(recv, recv_sem, 0)
    coefs = owned(0)
    call[mine] = coefs
    share(call.at[mine], call.at[mine], 0)

    def mix(chunk, total):
        keep = own_pair(chunk, 128)
        part = None
        for g in range(4):
            wide = dot(masked(coefs_at(call, mine, g), keep), tab["spread"][...])
            value = wide * weights_of(chunk, g)
            value = value[:, :128] + value[:, 128:]
            part = value if part is None else part + value
        high, low = split(part)
        value = dot(jnp.concatenate([high, low], axis=1), tab["to_modes"][...])
        return total + fold(value, own_pair(chunk, 512))

    mixed = lax.fori_loop(0, 4, mix, jnp.zeros((K, 512), F32))
    planes_out(1, mixed)
    exchange(1)

    wait_share(call, 0)

    def spread_member(step, carry):
        member, chunk = step // 4, lax.rem(step, 4)
        keep = own_pair(chunk, 128)
        for g in range(4):
            cexp[member, pl.ds(pl.multiple_of(chunk * 128, 128), 128), g * 256 : (g + 1) * 256] = dot(
                masked(coefs_at(call, member, g), keep), tab["spread"][...]
            )
        return carry

    lax.fori_loop(0, 4 * n_ens, spread_member, 0)

    wait_all(recv, recv_sem, 1)
    narrow(1)
    bsum[...] = jnp.zeros_like(bsum)

    def activate(step, carry):
        group, pair = step // 4, lax.rem(step, 4)
        both = dot(s2[group], tab["wide"][:, pl.ds(pl.multiple_of(pair * 256, 256), 256)])
        for half in range(2):
            o = step * 2 + half
            v = both[:, half * 128 : (half + 1) * 128] + pre[o] + bias[o]
            square = v * v
            t = jnp.tanh(ROOT * (v + 0.044715 * (v * square)))
            out_v[o] = (0.5 * v * (1.0 + t)).astype(BF)
            grad = 0.5 * (1.0 + t) + (0.5 * ROOT) * v * (1.0 - t * t) * (1.0 + (3 * 0.044715) * square)
            slope = (cot_v[o].astype(F32) * grad).astype(BF)
            slope_v[o] = slope
            bsum[pl.ds(32 + o, 1), :] = jnp.sum(slope.astype(F32), axis=0, keepdims=True)
        return carry

    lax.fori_loop(0, C // 2, activate, 0)
    stores = [pltpu.make_async_copy(out_v, out, store_sem.at[0])]
    stores[0].start()

    project(slope_v, 2)
    exchange(2)

    gacc[...] = jnp.zeros_like(gacc)

    def outer(at, carry):
        gacc[...] += dot_nt(block_of(field_v, at), block_of(slope_v, at))
        return carry

    lax.fori_loop(0, N // (2 * XB), outer, 0)
    same = lax.rem(lax.broadcasted_iota(jnp.int32, (512, 512), 0), XB) == lax.rem(
        lax.broadcasted_iota(jnp.int32, (512, 512), 1), XB
    )
    rows = jnp.sum(jnp.where(same, gacc[...], 0.0).reshape(C, XB, 512), axis=1)
    high, low = split(rows)
    grad_rows = dot(high, tab["lanes"][...]) + dot(low, tab["lanes"][...])
    high, low = split(bsum[...])
    ones = jnp.ones((8, 128), BF)
    bias_row = (dot_nt(ones, high) + dot_nt(ones, low))[0:1]
    glsend[:, 0, :] = grad_rows + bias_row
    spread_out(glsend, glrecv, 0, True)
    glrecv[slot(me)] = glsend[me // 2]
    pointwise(kl_b, slope_v)

    wait_all(recv, recv_sem, 2)
    back = owned(2)
    ball[mine] = back
    share(ball.at[mine], ball.at[mine], 1)

    def mix_back(chunk, total):
        keep = own_pair(chunk, 128)
        four = to_channels(ball[mine], keep)
        four = jnp.concatenate([four, four], axis=1)
        parts = []
        for g in range(4):
            high, low = split(weights_of(chunk, g) * four)
            value = dot(jnp.concatenate([high, low], axis=1), tab["gather"][...])
            parts.append(fold(value, keep))
        return total + jnp.concatenate(parts, axis=1)

    back_modes = lax.fori_loop(0, 4, mix_back, jnp.zeros((K, 512), F32))
    planes_out(3, back_modes)
    exchange(3)

    wait_block(glrecv, gl_recv, 0)
    glall[mine] = jnp.sum(glrecv[...], axis=0)
    share(glall.at[mine], glall.at[mine], 2)
    wait_share(ball, 1)
    wait_share(glall, 2)
    glfin_send[0] = glall[0] + glall[1] + glall[2] + glall[3]
    spread_out(glfin_send, glfin, 1, False)
    glfin[slot(me)] = glfin_send[0]

    def spectral(chunk, carry):
        keep = own_pair(chunk, 128)
        rows = pl.ds(pl.multiple_of(chunk * 128, 128), 128)
        fours = []
        for member in range(n_ens):
            four = to_channels(ball[member], keep)
            fours.append(jnp.concatenate([four, four], axis=1))
        for g in range(4):
            total = None
            for member in range(n_ens):
                part = cexp[member, rows, g * 256 : (g + 1) * 256] * fours[member]
                total = part if total is None else total + part
            gs_v[pl.ds(chunk * 4, 4), :, g * 256 : (g + 1) * 256] = total.reshape(4, 32, 256)
        return carry

    lax.fori_loop(0, 4, spectral, 0)
    stores.append(pltpu.make_async_copy(gs_v, gs, store_sem.at[1]))
    stores[1].start()

    wait_all(recv, recv_sem, 3)
    narrow(3)

    def finish(step, carry):
        group, pair = step // 4, lax.rem(step, 4)
        both = dot(s2[group], tab["wide"][:, pl.ds(pl.multiple_of(pair * 256, 256), 256)])
        for half in range(2):
            o = step * 2 + half
            gf_v[o] = (both[:, half * 128 : (half + 1) * 128] + pre[o]).astype(BF)
        return carry

    lax.fori_loop(0, C // 2, finish, 0)
    stores.append(pltpu.make_async_copy(gf_v, gf, store_sem.at[2]))
    stores[2].start()

    wait_block(glfin, gl_recv, 1)
    final = glfin[:32, 0, :]
    gl_out[...] = final[:, :32]
    gb_out[...] = final[0:1, 32:64]

    for phase in range(4):
        wait_all(send, send_sem, phase)
    wait_block(glrecv, gl_send, 0)
    wait_block(glfin, gl_send, 1)
    wait_share_sent(call, 0)
    wait_share_sent(ball, 1)
    wait_share_sent(glall, 2)
    for store in stores:
        store.wait()


def slot(device):
    return lax.rem(device, 2) * 32 + device // 2


def coefs_at(ref, member, g):
    return ref[member, :, g * 128 : (g + 1) * 128]


def wait_all(ref, sem, phase):
    some = ref.at[phase, pl.ds(0, NZ - 1)]
    pltpu.make_async_copy(some, some, sem.at[phase]).wait()


def wait_block(ref, sem, at):
    some = ref.at[pl.ds(0, NZ - 1)]
    pltpu.make_async_copy(some, some, sem.at[at]).wait()


def local(n_slab, n_ens, field, weight, local_weight, bias, cotangent):
    consts = [jnp.asarray(TABLES[name]) for name in NAMES]
    any_spec = pl.BlockSpec(memory_space=pl.ANY)
    vmem = pl.BlockSpec(memory_space=pltpu.VMEM)
    smem = pl.BlockSpec(memory_space=pltpu.SMEM)
    image = (C, N, N)
    dma = pltpu.SemaphoreType.DMA
    outs = pl.pallas_call(
        functools.partial(kernel, n_slab, n_ens),
        out_shape=(
            jax.ShapeDtypeStruct(image, BF),
            jax.ShapeDtypeStruct(image, BF),
            jax.ShapeDtypeStruct((16, 32, 1024), F32),
            jax.ShapeDtypeStruct((32, 32), F32),
            jax.ShapeDtypeStruct((1, 32), F32),
        ),
        in_specs=[any_spec, any_spec, vmem, smem, any_spec] + [any_spec] * len(NAMES),
        out_specs=(any_spec, any_spec, any_spec, vmem, vmem),
        scratch_shapes=[pltpu.VMEM(TABLES[name].shape, BF) for name in NAMES]
        + [
            pltpu.VMEM(image, BF),
            pltpu.VMEM(image, BF),
            pltpu.VMEM((16, 32, 1024), BF),
            pltpu.VMEM(image, F32),
            pltpu.VMEM(image, BF),
            pltpu.VMEM(image, BF),
            pltpu.VMEM(image, BF),
            pltpu.VMEM((16, 32, 1024), F32),
            pltpu.VMEM((512, 512), BF),
            pltpu.VMEM((512, 512), BF),
            pltpu.VMEM((4, 128, 256), BF),
            pltpu.VMEM((n_ens, 512, 1024), F32),
            pltpu.VMEM((512, 512), F32),
            pltpu.VMEM((128, 128), F32),
            pltpu.VMEM((4, NZ, 4, 128), F32),
            pltpu.VMEM((4, NZ, 4, 128), F32),
            pltpu.VMEM((n_ens, K, 512), F32),
            pltpu.VMEM((n_ens, K, 512), F32),
            pltpu.VMEM((32, 1, 128), F32),
            pltpu.VMEM((NZ, 1, 128), F32),
            pltpu.VMEM((n_ens, 1, 128), F32),
            pltpu.VMEM((1, 1, 128), F32),
            pltpu.VMEM((NZ, 1, 128), F32),
            dma((3,)),
            dma((3,)),
            dma((len(NAMES),)),
            dma((4,)),
            dma((4,)),
            dma((3,)),
            dma((3,)),
            dma((2,)),
            dma((2,)),
        ],
        compiler_params=pltpu.CompilerParams(
            collective_id=0, has_side_effects=True, vmem_limit_bytes=56 * 1024 * 1024
        ),
    )(
        field.reshape(image),
        weight,
        local_weight,
        bias,
        cotangent.reshape(image),
        *consts,
    )
    output, grad_field, grad_spectral, grad_local, grad_bias = outs
    whole = (1, 1) + image
    return (
        output.reshape(whole),
        grad_field.reshape(whole),
        grad_spectral,
        grad_local,
        grad_bias.reshape(32),
    )


def solution(mesh):
    placed = (
        P("ens", "slab", None, None, None),
        P("slab", None, None),
        P(),
        P(),
        P("ens", "slab", None, None, None),
    )
    return jax.shard_map(
        functools.partial(local, mesh.shape["slab"], mesh.shape["ens"]),
        mesh=mesh,
        in_specs=placed,
        out_specs=(
            P("ens", "slab", None, None, None),
            P("ens", "slab", None, None, None),
            P("slab", None, None),
            P(),
            P(),
        ),
        check_vma=False,
    )
```

time: 724 us -> 63.5 us (0.09)
  waiting for transfers between devices: 511 us -> 0 us
  blocking collectives: 80.8 us -> 0 us
  matrix products: 64.7 us -> 0 us
  Pallas kernels: 0 us -> 56.8 us
  other arithmetic: 23.9 us -> 0 us
  local copies, waits for them, and re-layouts: 22.9 us -> 5.88 us
  between operations: 14.2 us -> 0.66 us
    reduce_scatter x2 -> x0, waiting for transfers between devices: 365 us -> none  [project(): lax.psum_scatter(partial_modes, 'slab', scatter_dimension=3, tiled=True)]
    all_gather x2 -> x0, waiting for transfers between devices: 103 us -> none  [synthesize(): lax.all_gather(coefs, 'slab', axis=3, tiled=True)]
    psum x1 -> x0, blocking collectives: 80.8 us -> none  [local(): grad_local, grad_bias = lax.psum((local_part, bias_part), ('slab', 'ens'))]
    dot_general x13 -> x0, matrix products: 62.2 us -> none  [the longest x2 22 us: synthesize(): jnp.einsum('mkcp,kz->mzcp', lax.all_gather(coefs, 'slab', axis=3, tiled=T...]
    pallas_call x0 -> x1, Pallas kernels: none -> 56.8 us  [local(): pl.pallas_call(functools.partial(kernel, n_slab, n_ens), out_shape=(jax.S...]
    psum x1 -> x0, waiting for transfers between devices: 42.5 us -> none  [local(): grad_mixing = lax.psum(mixing_part, 'ens')]
    transpose x2 -> x0, other arithmetic: 16 us -> none  [project(): jnp.einsum('mzcp,kz->mkcp', along_x, basis_local, precision=highest)]
    reshape x2 -> x0, local copies, waits for them, and re-layouts: 12 us -> none  [the longest x1 7.69 us: local(): grad_mixing.reshape(pairs, modes, channels * channels)]
  transfers between devices with their start and end apart: 5 -> 0, of which waited for: 5 -> 0; matrix products, arithmetic and copies ran while one was open for 7% -> 0% of each run, Pallas kernels for 0% -> 0%
where the time goes in v1:
time: 63.5 us; the launch traced here: 63.3 us
  Pallas kernels  56.8 us (89%)
  local copies, waits for them, and re-layouts  5.88 us (9%)
  between operations  0.66 us (1%)
    pallas_call x1, Pallas kernels, local(): pl.pallas_call(functools.partial(kernel, n_slab, n_ens), out_shape=(jax.S...  56.8 us
    unnamed x13, local copies, waits for them, and re-layouts  5.88 us

profile of v1, /device:TPU:1, one launch (start us, length us, event | category | flops | bytes accessed | tf_op | source)
XLA Modules:
  0.0 63.3 jit_solution(4027370015592268241)
XLA Ops:
  0.6 56.8 %shard_map.209 = (bf16[32,128,128]{2,1,0:T(8,128)(2,1)}, bf16[32,128,128]{2,1,0:T(8,128)(2,1)}, f32[16,32,1024]{2,1,0:T(8,128)}, f32[32,32]{1,0:T(8,128)}, f32[1,32]{1,0:T(1,128)}) custom-call(bf16[32,128,128]{2,1,0:T(8,128)(2,1)} %bitcast.7, bf16[16,32,1024]{2,1,0:T(8,128)(2,1)} %weight.1, bf16[32,32]{1,0:T(8,128)(2,1)} %lw.1, f32[32]{0:T(128)} %bias.1, ...), custom_call_target="tpu_custom_call" | custom-call | tf_op jit(solution)/shard_map/pallas_call | solution.py:460
  57.4 0.0 copy-start.1
  57.4 0.0 copy-start
  57.4 2.5 %copy.28 = bf16[1,1,32,128,128]{4,3,2,1,0:T(8,128)(2,1)} copy(bf16[1,1,32,128,128]{4,3,2,1,0:T(8,128)(2,1)} %bitcast.6) | data formatting | bytes 2097152
  59.9 0.0 copy-done.1
  59.9 1.0 %copy.29 = bf16[1,1,32,128,128]{4,3,2,1,0:T(8,128)(2,1)} copy(bf16[1,1,32,128,128]{4,3,2,1,0:T(8,128)(2,1)S(1)} %bitcast.5) | data formatting | bytes 2097152
  60.9 0.0 copy-done
  60.9 0.0 copy-start.2
  60.9 0.0 copy-start.3
  60.9 1.3 %copy.30 = f32[16,32,1024]{2,1,0:T(8,128)} copy(f32[16,32,1024]{2,1,0:T(8,128)S(1)} %copy-done) | data formatting | bytes 4194304
  62.2 0.0 copy-done.2
  62.2 0.6 copy.31
  62.8 0.0 copy-done.3
  62.8 0.5 copy.32
Async XLA Ops:
  57.4 2.5 %copy-start.1 = (bf16[32,128,128]{2,1,0:T(8,128)(2,1)S(1)}, bf16[32,128,128]{2,1,0:T(8,128)(2,1)}, u32[]{:S(2)}) copy-start(bf16[32,128,128]{2,1,0:T(8,128)(2,1)} %get-tuple-element.11) | copy-start | bytes 3145732
  57.4 3.4 %copy-start = (f32[16,32,1024]{2,1,0:T(8,128)S(1)}, f32[16,32,1024]{2,1,0:T(8,128)}, u32[]{:S(2)}) copy-start(f32[16,32,1024]{2,1,0:T(8,128)} %get-tuple-element.22) | copy-start | bytes 6291460
  60.9 1.3 %copy-start.2 = (f32[32,32]{1,0:T(8,128)S(1)}, f32[32,32]{1,0:T(8,128)}, u32[]{:S(2)}) copy-start(f32[32,32]{1,0:T(8,128)} %get-tuple-element.23) | copy-start | bytes 12292
  60.9 1.9 %copy-start.3 = (f32[1,32]{1,0:T(1,128)S(1)}, f32[1,32]{1,0:T(1,128)}, u32[]{:S(2)}) copy-start(f32[1,32]{1,0:T(1,128)} %get-tuple-element.14) | copy-start | bytes 388

commit v2 on v1

--- a/solution.py
+++ b/solution.py
@@ -54,8 +54,7 @@
     to_modes = np.tile(np.repeat(eye32, 16, axis=1), (4, 1))
     from_modes = to_modes.T.reshape(4, 128, 128)
     rows = np.repeat(eye32, XB, axis=0)
-    lanes = np.zeros((512, 128), np.float32)
-    lanes[:, :32] = rows
+    lanes = np.tile(rows, (1, 4))
     return dict(
         wide_t=wide.T.copy(),
         bx=three(basis),
@@ -95,6 +94,16 @@
     return dot(table, jnp.concatenate([high, low, high], axis=0))
 
 
+def middle_out(at, size):
+    return size // 2 + (at + 1) // 2 * (2 * lax.rem(at + 1, 2) - 1)
+
+
+def far_first(me, at):
+    x = lax.rem(me // 16 + middle_out(lax.rem(at // 2, 4), 4), 4)
+    z = lax.rem(lax.rem(me // 2, 8) + middle_out(at // 8, 8), 8)
+    return x * 16 + z * 2 + lax.rem(me + 1 + at, 2)
+
+
 def kernel(n_slab, n_ens, field, weight, lw, bias, cot, *rest):
     consts = dict(zip(NAMES, rest[: len(NAMES)]))
     rest = rest[len(NAMES) :]
@@ -103,12 +112,23 @@
     tab = dict(zip(NAMES, rest[: len(NAMES)]))
     rest = rest[len(NAMES) :]
     (
-        field_v, cot_v, w_v, pre, out_v, slope_v, gf_v, gs_v, kl_f, kl_b, s2, cexp, gacc, bsum,
-        send, recv, call, ball, glsend, glrecv, glall, glfin_send, glfin,
-        load_sem, store_sem, tab_sem, send_sem, recv_sem, ens_send, ens_recv, gl_send, gl_recv,
+        field_v, cot_v, w_v, pre, out_v, slope_v, gf_v, gs_v, kl_f, kl_b, cexp, gacc,
+        send, recv, call, ball, sums,
+        load_sem, store_sem, tab_sem, send_sem, recv_sem, ens_send, ens_recv, sum_send, sum_recv,
     ) = rest
     me = lax.axis_index("slab")
     mine = lax.axis_index("ens")
+    x, z, core = me // 16, lax.rem(me // 2, 8), lax.rem(me, 2)
+
+    barrier = pltpu.get_barrier_semaphore()
+
+    def greet(at, carry):
+        pl.semaphore_signal(barrier, inc=1, device_id={"slab": lax.rem(me + at, n_slab)}, device_id_type=MESH)
+        return carry
+
+    lax.fori_loop(1, n_slab, greet, 0)
+    for at in range(1, n_ens):
+        pl.semaphore_signal(barrier, inc=1, device_id={"ens": lax.rem(mine + at, n_ens)}, device_id_type=MESH)
 
     loads = [
         pltpu.make_async_copy(field, field_v, load_sem.at[0]),
@@ -126,33 +146,12 @@
     loads[1].start()
     loads[2].start()
 
-    barrier = pltpu.get_barrier_semaphore()
-
-    def greet(at, carry):
-        pl.semaphore_signal(barrier, inc=1, device_id={"slab": lax.rem(me + at, n_slab)}, device_id_type=MESH)
-        return carry
-
-    lax.fori_loop(1, n_slab, greet, 0)
-    for at in range(1, n_ens):
-        pl.semaphore_signal(barrier, inc=1, device_id={"ens": lax.rem(mine + at, n_ens)}, device_id_type=MESH)
-
-    def project(data, phase):
-        for g in range(4):
-            total = None
-            for pair in range(4):
-                at = g * 8 + pair * 2
-                part = dot(
-                    jnp.concatenate([data[at], data[at + 1]], axis=1),
-                    tab["wide_t"][pair * 256 : (pair + 1) * 256, :],
-                )
-                total = part if total is None else total + part
-            modes = dot_three(tab["bx"][...], total)
-            send[phase, :32, g, :] = modes[:, :128]
-            send[phase, 32:, g, :] = modes[:, 128:]
+    def project(data, pair):
+        return dot(jnp.concatenate(data, axis=1), tab["wide_t"][pair * 256 : (pair + 1) * 256, :])
 
     def exchange(phase):
         def one(at, carry):
-            peer = lax.rem(me + at, n_slab)
+            peer = far_first(me, at)
             pltpu.make_async_remote_copy(
                 src_ref=send.at[phase, slot(peer)],
                 dst_ref=recv.at[phase, slot(me)],
@@ -163,7 +162,7 @@
             ).start()
             return carry
 
-        lax.fori_loop(1, n_slab, one, 0)
+        lax.fori_loop(0, n_slab - 1, one, 0)
         recv[phase, slot(me)] = send[phase, slot(me)]
 
     def share(source, target, at_sem):
@@ -185,20 +184,20 @@
         some = ref.at[pl.ds(0, n_ens - 1)]
         pltpu.make_async_copy(some, some, ens_send.at[at_sem]).wait()
 
-    def spread_out(source, target, at_sem, row):
-        def one(at, carry):
-            peer = lax.rem(me + at, n_slab)
+    def share_sums(stage, place, peers):
+        for peer in peers:
             pltpu.make_async_remote_copy(
-                src_ref=source.at[peer // 2] if row else source.at[0],
-                dst_ref=target.at[slot(me)],
-                send_sem=gl_send.at[at_sem],
-                recv_sem=gl_recv.at[at_sem],
-                device_id={"slab": peer},
+                src_ref=sums.at[stage, place],
+                dst_ref=sums.at[stage, place],
+                send_sem=sum_send.at[stage],
+                recv_sem=sum_recv.at[stage],
+                device_id=peer,
                 device_id_type=MESH,
             ).start()
-            return carry
-
-        lax.fori_loop(1, n_slab, one, 0)
+
+    def wait_sums(stage, size, sem):
+        some = sums.at[stage, pl.ds(0, size - 1)]
+        pltpu.make_async_copy(some, some, sem.at[stage]).wait()
 
     def owned(phase):
         planes = jnp.concatenate([recv[phase, :, g, :] for g in range(4)], axis=1)
@@ -233,10 +232,14 @@
     def weights_of(chunk, g):
         return w_v[pl.ds(chunk * 4, 4), :, g * 256 : (g + 1) * 256].reshape(128, 256).astype(F32)
 
-    def narrow(phase):
-        for g in range(4):
-            modes = jnp.concatenate([recv[phase, :32, g, :], recv[phase, 32:, g, :]], axis=1)
-            s2[g] = dot_three(tab["bxt"][...], modes).astype(BF)
+    def narrow(phase, g):
+        modes = jnp.concatenate([recv[phase, :32, g, :], recv[phase, 32:, g, :]], axis=1)
+        return dot_three(tab["bxt"][...], modes).astype(BF)
+
+    def put(phase, g, total):
+        modes = dot_three(tab["bx"][...], total)
+        send[phase, :32, g, :] = modes[:, :128]
+        send[phase, 32:, g, :] = modes[:, 128:]
 
     def block_of(ref, at):
         a = ref[:, pl.ds(pl.multiple_of(at * 2 * XB, 2 * XB), XB), :].reshape(C * XB, N)
@@ -255,7 +258,13 @@
     tab_loads["wide_t"].wait()
     tab_loads["bx"].wait()
     loads[0].wait()
-    project(field_v, 0)
+    for g in range(4):
+        total = None
+        for pair in range(4):
+            at = g * 8 + pair * 2
+            part = project([field_v[at], field_v[at + 1]], pair)
+            total = part if total is None else total + part
+        put(0, g, total)
     pl.semaphore_wait(barrier, n_slab - 1 + n_ens - 1)
     exchange(0)
 
@@ -275,7 +284,6 @@
     wait_all(recv, recv_sem, 0)
     coefs = owned(0)
     call[mine] = coefs
-    share(call.at[mine], call.at[mine], 0)
 
     def mix(chunk, total):
         keep = own_pair(chunk, 128)
@@ -289,69 +297,78 @@
         value = dot(jnp.concatenate([high, low], axis=1), tab["to_modes"][...])
         return total + fold(value, own_pair(chunk, 512))
 
-    mixed = lax.fori_loop(0, 4, mix, jnp.zeros((K, 512), F32))
+    mixed = lax.fori_loop(0, 4, mix, jnp.zeros((K, 512), F32), unroll=True)
     planes_out(1, mixed)
     exchange(1)
 
-    wait_share(call, 0)
-
-    def spread_member(step, carry):
-        member, chunk = step // 4, lax.rem(step, 4)
-        keep = own_pair(chunk, 128)
-        for g in range(4):
-            cexp[member, pl.ds(pl.multiple_of(chunk * 128, 128), 128), g * 256 : (g + 1) * 256] = dot(
-                masked(coefs_at(call, member, g), keep), tab["spread"][...]
-            )
+
+    def spread_member(at, carry):
+        member = lax.rem(mine + at, n_ens)
+        for chunk in range(4):
+            keep = own_pair(chunk, 128)
+            for g in range(4):
+                cexp[member, chunk * 128 : (chunk + 1) * 128, g * 256 : (g + 1) * 256] = dot(
+                    masked(coefs_at(call, member, g), keep), tab["spread"][...]
+                )
         return carry
 
-    lax.fori_loop(0, 4 * n_ens, spread_member, 0)
+    spread_member(0, 0)
 
     wait_all(recv, recv_sem, 1)
-    narrow(1)
-    bsum[...] = jnp.zeros_like(bsum)
-
-    def activate(step, carry):
-        group, pair = step // 4, lax.rem(step, 4)
-        both = dot(s2[group], tab["wide"][:, pl.ds(pl.multiple_of(pair * 256, 256), 256)])
-        for half in range(2):
-            o = step * 2 + half
-            v = both[:, half * 128 : (half + 1) * 128] + pre[o] + bias[o]
-            square = v * v
-            t = jnp.tanh(ROOT * (v + 0.044715 * (v * square)))
-            out_v[o] = (0.5 * v * (1.0 + t)).astype(BF)
-            grad = 0.5 * (1.0 + t) + (0.5 * ROOT) * v * (1.0 - t * t) * (1.0 + (3 * 0.044715) * square)
-            slope = (cot_v[o].astype(F32) * grad).astype(BF)
-            slope_v[o] = slope
-            bsum[pl.ds(32 + o, 1), :] = jnp.sum(slope.astype(F32), axis=0, keepdims=True)
-        return carry
-
-    lax.fori_loop(0, C // 2, activate, 0)
+    share(call.at[mine], call.at[mine], 0)
+    for g in range(4):
+        narrowed = narrow(1, g)
+        total = None
+        for pair in range(4):
+            both = dot(narrowed, tab["wide"][:, pair * 256 : (pair + 1) * 256])
+            slopes = []
+            for half in range(2):
+                o = g * 8 + pair * 2 + half
+                v = both[:, half * 128 : (half + 1) * 128] + (pre[o] + bias[o])
+                cubic = (ROOT * 0.044715) * (v * v)
+                t = jnp.tanh(v * (ROOT + cubic))
+                h = 0.5 * v
+                out_v[o] = (h + h * t).astype(BF)
+                grad = (0.5 + 0.5 * t) + (h * (1.0 - t * t)) * (ROOT + 3.0 * cubic)
+                slopes.append((cot_v[o].astype(F32) * grad).astype(BF))
+                slope_v[o] = slopes[-1]
+            part = project(slopes, pair)
+            total = part if total is None else total + part
+        put(2, g, total)
+    exchange(2)
     stores = [pltpu.make_async_copy(out_v, out, store_sem.at[0])]
     stores[0].start()
 
-    project(slope_v, 2)
-    exchange(2)
-
     gacc[...] = jnp.zeros_like(gacc)
 
     def outer(at, carry):
-        gacc[...] += dot_nt(block_of(field_v, at), block_of(slope_v, at))
+        ones = jnp.ones((XB, 2 * N), BF)
+        gacc[...] += dot_nt(jnp.concatenate([block_of(field_v, at), ones], axis=0), block_of(slope_v, at))
         return carry
 
     lax.fori_loop(0, N // (2 * XB), outer, 0)
     same = lax.rem(lax.broadcasted_iota(jnp.int32, (512, 512), 0), XB) == lax.rem(
         lax.broadcasted_iota(jnp.int32, (512, 512), 1), XB
     )
-    rows = jnp.sum(jnp.where(same, gacc[...], 0.0).reshape(C, XB, 512), axis=1)
-    high, low = split(rows)
-    grad_rows = dot(high, tab["lanes"][...]) + dot(low, tab["lanes"][...])
-    high, low = split(bsum[...])
-    ones = jnp.ones((8, 128), BF)
-    bias_row = (dot_nt(ones, high) + dot_nt(ones, low))[0:1]
-    glsend[:, 0, :] = grad_rows + bias_row
-    spread_out(glsend, glrecv, 0, True)
-    glrecv[slot(me)] = glsend[me // 2]
+    rows = jnp.sum(jnp.where(same, gacc[: C * XB], 0.0).reshape(C, XB, 512), axis=1)
+    bias_rows = gacc[C * XB : C * XB + XB]
+    high, low = split(jnp.concatenate([rows, bias_rows], axis=0))
+    rows = dot(high, tab["lanes"][...]) + dot(low, tab["lanes"][...])
+    lane = lax.broadcasted_iota(jnp.int32, (8, 128), 1) // 32
+    packed = jnp.zeros((8, 128), F32)
+    for part in range(4):
+        packed = packed + jnp.where(lane == part, rows[part * 8 : (part + 1) * 8], 0.0)
+    near = x * 2 + core
+    sums[0, near, :8] = packed
+    sums[0, near, 8:] = rows[C : C + 8]
+    peers = [lax.rem(near + at, 8) for at in range(1, 8)]
+    share_sums(0, near, [{"slab": peer // 2 * 16 + z * 2 + lax.rem(peer, 2)} for peer in peers])
     pointwise(kl_b, slope_v)
+    wait_share(call, 0)
+    lax.fori_loop(1, n_ens, spread_member, 0)
+    wait_sums(0, 8, sum_recv)
+    sums[1, z] = jnp.sum(sums[0], axis=0)
+    share_sums(1, z, [{"slab": x * 16 + lax.rem(z + at, 8) * 2 + core} for at in range(1, 8)])
 
     wait_all(recv, recv_sem, 2)
     back = owned(2)
@@ -369,18 +386,15 @@
             parts.append(fold(value, keep))
         return total + jnp.concatenate(parts, axis=1)
 
-    back_modes = lax.fori_loop(0, 4, mix_back, jnp.zeros((K, 512), F32))
+    back_modes = lax.fori_loop(0, 4, mix_back, jnp.zeros((K, 512), F32), unroll=True)
     planes_out(3, back_modes)
     exchange(3)
 
-    wait_block(glrecv, gl_recv, 0)
-    glall[mine] = jnp.sum(glrecv[...], axis=0)
-    share(glall.at[mine], glall.at[mine], 2)
+
+    wait_sums(1, 8, sum_recv)
+    sums[2, mine] = jnp.sum(sums[1], axis=0)
+    share_sums(2, mine, [{"ens": lax.rem(mine + at, n_ens)} for at in range(1, n_ens)])
     wait_share(ball, 1)
-    wait_share(glall, 2)
-    glfin_send[0] = glall[0] + glall[1] + glall[2] + glall[3]
-    spread_out(glfin_send, glfin, 1, False)
-    glfin[slot(me)] = glfin_send[0]
 
     def spectral(chunk, carry):
         keep = own_pair(chunk, 128)
@@ -402,32 +416,28 @@
     stores[1].start()
 
     wait_all(recv, recv_sem, 3)
-    narrow(3)
-
-    def finish(step, carry):
-        group, pair = step // 4, lax.rem(step, 4)
-        both = dot(s2[group], tab["wide"][:, pl.ds(pl.multiple_of(pair * 256, 256), 256)])
-        for half in range(2):
-            o = step * 2 + half
-            gf_v[o] = (both[:, half * 128 : (half + 1) * 128] + pre[o]).astype(BF)
-        return carry
-
-    lax.fori_loop(0, C // 2, finish, 0)
+    for g in range(4):
+        narrowed = narrow(3, g)
+        for pair in range(4):
+            both = dot(narrowed, tab["wide"][:, pair * 256 : (pair + 1) * 256])
+            for half in range(2):
+                o = g * 8 + pair * 2 + half
+                gf_v[o] = (both[:, half * 128 : (half + 1) * 128] + pre[o]).astype(BF)
     stores.append(pltpu.make_async_copy(gf_v, gf, store_sem.at[2]))
     stores[2].start()
 
-    wait_block(glfin, gl_recv, 1)
-    final = glfin[:32, 0, :]
-    gl_out[...] = final[:, :32]
-    gb_out[...] = final[0:1, 32:64]
+    wait_sums(2, n_ens, sum_recv)
+    total = sums[2, 0] + sums[2, 1] + sums[2, 2] + sums[2, 3]
+    for part in range(4):
+        gl_out[part * 8 : (part + 1) * 8, :] = total[:8, part * 32 : (part + 1) * 32]
+    gb_out[...] = total[8:9, :32]
 
     for phase in range(4):
         wait_all(send, send_sem, phase)
-    wait_block(glrecv, gl_send, 0)
-    wait_block(glfin, gl_send, 1)
+    for stage, size in enumerate((8, 8, n_ens)):
+        wait_sums(stage, size, sum_send)
     wait_share_sent(call, 0)
     wait_share_sent(ball, 1)
-    wait_share_sent(glall, 2)
     for store in stores:
         store.wait()
 
@@ -443,11 +453,6 @@
 def wait_all(ref, sem, phase):
     some = ref.at[phase, pl.ds(0, NZ - 1)]
     pltpu.make_async_copy(some, some, sem.at[phase]).wait()
-
-
-def wait_block(ref, sem, at):
-    some = ref.at[pl.ds(0, NZ - 1)]
-    pltpu.make_async_copy(some, some, sem.at[at]).wait()
 
 
 def local(n_slab, n_ens, field, weight, local_weight, bias, cotangent):
@@ -480,28 +485,22 @@
             pltpu.VMEM((16, 32, 1024), F32),
             pltpu.VMEM((512, 512), BF),
             pltpu.VMEM((512, 512), BF),
-            pltpu.VMEM((4, 128, 256), BF),
             pltpu.VMEM((n_ens, 512, 1024), F32),
-            pltpu.VMEM((512, 512), F32),
-            pltpu.VMEM((128, 128), F32),
+            pltpu.VMEM((512 + XB, 512), F32),
             pltpu.VMEM((4, NZ, 4, 128), F32),
             pltpu.VMEM((4, NZ, 4, 128), F32),
             pltpu.VMEM((n_ens, K, 512), F32),
             pltpu.VMEM((n_ens, K, 512), F32),
-            pltpu.VMEM((32, 1, 128), F32),
-            pltpu.VMEM((NZ, 1, 128), F32),
-            pltpu.VMEM((n_ens, 1, 128), F32),
-            pltpu.VMEM((1, 1, 128), F32),
-            pltpu.VMEM((NZ, 1, 128), F32),
+            pltpu.VMEM((3, 8, 16, 128), F32),
             dma((3,)),
             dma((3,)),
             dma((len(NAMES),)),
             dma((4,)),
             dma((4,)),
+            dma((2,)),
+            dma((2,)),
             dma((3,)),
             dma((3,)),
-            dma((2,)),
-            dma((2,)),
         ],
         compiler_params=pltpu.CompilerParams(
             collective_id=0, has_side_effects=True, vmem_limit_bytes=56 * 1024 * 1024

time: 63.5 us -> 56.9 us (0.90)
  Pallas kernels: 56.8 us -> 50.2 us
    pallas_call x1, Pallas kernels: 56.8 us -> 50.2 us  [local(): pl.pallas_call(functools.partial(kernel, n_slab, n_ens), out_shape=(jax.S...]
where the time goes in v2:
time: 56.9 us; the launch traced here: 56.8 us
  Pallas kernels  50.2 us (88%)
  local copies, waits for them, and re-layouts  5.88 us (10%)
  between operations  0.66 us (1%)
    pallas_call x1, Pallas kernels, local(): pl.pallas_call(functools.partial(kernel, n_slab, n_ens), out_shape=(jax.S...  50.2 us
    unnamed x13, local copies, waits for them, and re-layouts  5.88 us

profile of v2, /device:TPU:1, one launch (start us, length us, event | category | flops | bytes accessed | tf_op | source)
XLA Modules:
  0.0 56.8 jit_solution(10939416191691372200)
XLA Ops:
  0.6 50.2 %shard_map.209 = (bf16[32,128,128]{2,1,0:T(8,128)(2,1)}, bf16[32,128,128]{2,1,0:T(8,128)(2,1)}, f32[16,32,1024]{2,1,0:T(8,128)}, f32[32,32]{1,0:T(8,128)}, f32[1,32]{1,0:T(1,128)}) custom-call(bf16[32,128,128]{2,1,0:T(8,128)(2,1)} %bitcast.7, bf16[16,32,1024]{2,1,0:T(8,128)(2,1)} %weight.1, bf16[32,32]{1,0:T(8,128)(2,1)} %lw.1, f32[32]{0:T(128)} %bias.1, ...), custom_call_target="tpu_custom_call" | custom-call | tf_op jit(solution)/shard_map/pallas_call | solution.py:465
  50.9 0.0 copy-start.1
  50.9 0.0 copy-start
  50.9 2.5 %copy.28 = bf16[1,1,32,128,128]{4,3,2,1,0:T(8,128)(2,1)} copy(bf16[1,1,32,128,128]{4,3,2,1,0:T(8,128)(2,1)} %bitcast.6) | data formatting | bytes 2097152
  53.3 0.0 copy-done.1
  53.3 1.0 %copy.29 = bf16[1,1,32,128,128]{4,3,2,1,0:T(8,128)(2,1)} copy(bf16[1,1,32,128,128]{4,3,2,1,0:T(8,128)(2,1)S(1)} %bitcast.5) | data formatting | bytes 2097152
  54.3 0.0 copy-done
  54.3 0.0 copy-start.2
  54.3 0.0 copy-start.3
  54.3 1.3 %copy.30 = f32[16,32,1024]{2,1,0:T(8,128)} copy(f32[16,32,1024]{2,1,0:T(8,128)S(1)} %copy-done) | data formatting | bytes 4194304
  55.6 0.0 copy-done.2
  55.6 0.6 %copy.31 = f32[32,32]{1,0:T(8,128)} copy(f32[32,32]{1,0:T(8,128)S(1)} %copy-done.2) | data formatting | bytes 8192
  56.2 0.0 copy-done.3
  56.2 0.5 copy.32
Async XLA Ops:
  50.9 2.5 %copy-start.1 = (bf16[32,128,128]{2,1,0:T(8,128)(2,1)S(1)}, bf16[32,128,128]{2,1,0:T(8,128)(2,1)}, u32[]{:S(2)}) copy-start(bf16[32,128,128]{2,1,0:T(8,128)(2,1)} %get-tuple-element.11) | copy-start | bytes 3145732
  50.9 3.4 %copy-start = (f32[16,32,1024]{2,1,0:T(8,128)S(1)}, f32[16,32,1024]{2,1,0:T(8,128)}, u32[]{:S(2)}) copy-start(f32[16,32,1024]{2,1,0:T(8,128)} %get-tuple-element.22) | copy-start | bytes 6291460
  54.3 1.3 %copy-start.2 = (f32[32,32]{1,0:T(8,128)S(1)}, f32[32,32]{1,0:T(8,128)}, u32[]{:S(2)}) copy-start(f32[32,32]{1,0:T(8,128)} %get-tuple-element.23) | copy-start | bytes 12292
  54.3 1.9 %copy-start.3 = (f32[1,32]{1,0:T(1,128)S(1)}, f32[1,32]{1,0:T(1,128)}, u32[]{:S(2)}) copy-start(f32[1,32]{1,0:T(1,128)} %get-tuple-element.14) | copy-start | bytes 388

commit v3 on v2

--- a/solution.py
+++ b/solution.py
@@ -107,14 +107,14 @@
 def kernel(n_slab, n_ens, field, weight, lw, bias, cot, *rest):
     consts = dict(zip(NAMES, rest[: len(NAMES)]))
     rest = rest[len(NAMES) :]
-    out, gf, gs, gl_out, gb_out = rest[:5]
+    out_v, gs_v, pre, s2, total_out = rest[:5]
     rest = rest[5:]
     tab = dict(zip(NAMES, rest[: len(NAMES)]))
     rest = rest[len(NAMES) :]
     (
-        field_v, cot_v, w_v, pre, out_v, slope_v, gf_v, gs_v, kl_f, kl_b, cexp, gacc,
+        field_v, cot_v, w_v, slope_v, kl_f, kl_b, cexp, gacc,
         send, recv, call, ball, sums,
-        load_sem, store_sem, tab_sem, send_sem, recv_sem, ens_send, ens_recv, sum_send, sum_recv,
+        load_sem, tab_sem, send_sem, recv_sem, ens_send, ens_recv, sum_send, sum_recv,
     ) = rest
     me = lax.axis_index("slab")
     mine = lax.axis_index("ens")
@@ -336,8 +336,6 @@
             total = part if total is None else total + part
         put(2, g, total)
     exchange(2)
-    stores = [pltpu.make_async_copy(out_v, out, store_sem.at[0])]
-    stores[0].start()
 
     gacc[...] = jnp.zeros_like(gacc)
 
@@ -412,25 +410,12 @@
         return carry
 
     lax.fori_loop(0, 4, spectral, 0)
-    stores.append(pltpu.make_async_copy(gs_v, gs, store_sem.at[1]))
-    stores[1].start()
 
     wait_all(recv, recv_sem, 3)
     for g in range(4):
-        narrowed = narrow(3, g)
-        for pair in range(4):
-            both = dot(narrowed, tab["wide"][:, pair * 256 : (pair + 1) * 256])
-            for half in range(2):
-                o = g * 8 + pair * 2 + half
-                gf_v[o] = (both[:, half * 128 : (half + 1) * 128] + pre[o]).astype(BF)
-    stores.append(pltpu.make_async_copy(gf_v, gf, store_sem.at[2]))
-    stores[2].start()
-
+        s2[g] = narrow(3, g)
     wait_sums(2, n_ens, sum_recv)
-    total = sums[2, 0] + sums[2, 1] + sums[2, 2] + sums[2, 3]
-    for part in range(4):
-        gl_out[part * 8 : (part + 1) * 8, :] = total[:8, part * 32 : (part + 1) * 32]
-    gb_out[...] = total[8:9, :32]
+    total_out[...] = sums[2, 0] + sums[2, 1] + sums[2, 2] + sums[2, 3]
 
     for phase in range(4):
         wait_all(send, send_sem, phase)
@@ -438,6 +423,24 @@
         wait_sums(stage, size, sum_send)
     wait_share_sent(call, 0)
     wait_share_sent(ball, 1)
+
+
+def finish_kernel(out_v, gs_v, pre, s2, total, wide, out, gf, gs, gl_out, gb_out, gf_v, sems):
+    stores = [pltpu.make_async_copy(out_v, out, sems.at[4]), pltpu.make_async_copy(gs_v, gs, sems.at[5])]
+    for store in stores:
+        store.start()
+    for g in range(4):
+        for pair in range(4):
+            both = dot(s2[g], wide[:, pair * 256 : (pair + 1) * 256])
+            for half in range(2):
+                o = g * 8 + pair * 2 + half
+                gf_v[o] = (both[:, half * 128 : (half + 1) * 128] + pre[o]).astype(BF)
+        some = pl.ds(g * 8, 8)
+        stores.append(pltpu.make_async_copy(gf_v.at[some], gf.at[some], sems.at[g]))
+        stores[-1].start()
+    for part in range(4):
+        gl_out[part * 8 : (part + 1) * 8, :] = total[:8, part * 32 : (part + 1) * 32]
+    gb_out[...] = total[8:9, :32]
     for store in stores:
         store.wait()
 
@@ -462,27 +465,23 @@
     smem = pl.BlockSpec(memory_space=pltpu.SMEM)
     image = (C, N, N)
     dma = pltpu.SemaphoreType.DMA
-    outs = pl.pallas_call(
+    held = pl.pallas_call(
         functools.partial(kernel, n_slab, n_ens),
         out_shape=(
-            jax.ShapeDtypeStruct(image, BF),
-            jax.ShapeDtypeStruct(image, BF),
-            jax.ShapeDtypeStruct((16, 32, 1024), F32),
-            jax.ShapeDtypeStruct((32, 32), F32),
-            jax.ShapeDtypeStruct((1, 32), F32),
+            pltpu.VMEM(image, BF),
+            pltpu.VMEM((16, 32, 1024), F32),
+            pltpu.VMEM(image, F32),
+            pltpu.VMEM((4, 128, 256), BF),
+            pltpu.VMEM((16, 128), F32),
         ),
         in_specs=[any_spec, any_spec, vmem, smem, any_spec] + [any_spec] * len(NAMES),
-        out_specs=(any_spec, any_spec, any_spec, vmem, vmem),
+        out_specs=(vmem,) * 5,
         scratch_shapes=[pltpu.VMEM(TABLES[name].shape, BF) for name in NAMES]
         + [
             pltpu.VMEM(image, BF),
             pltpu.VMEM(image, BF),
             pltpu.VMEM((16, 32, 1024), BF),
-            pltpu.VMEM(image, F32),
             pltpu.VMEM(image, BF),
-            pltpu.VMEM(image, BF),
-            pltpu.VMEM(image, BF),
-            pltpu.VMEM((16, 32, 1024), F32),
             pltpu.VMEM((512, 512), BF),
             pltpu.VMEM((512, 512), BF),
             pltpu.VMEM((n_ens, 512, 1024), F32),
@@ -493,7 +492,6 @@
             pltpu.VMEM((n_ens, K, 512), F32),
             pltpu.VMEM((3, 8, 16, 128), F32),
             dma((3,)),
-            dma((3,)),
             dma((len(NAMES),)),
             dma((4,)),
             dma((4,)),
@@ -503,7 +501,7 @@
             dma((3,)),
         ],
         compiler_params=pltpu.CompilerParams(
-            collective_id=0, has_side_effects=True, vmem_limit_bytes=56 * 1024 * 1024
+            collective_id=0, has_side_effects=True, vmem_limit_bytes=57 * 1024 * 1024
         ),
     )(
         field.reshape(image),
@@ -513,7 +511,21 @@
         cotangent.reshape(image),
         *consts,
     )
-    output, grad_field, grad_spectral, grad_local, grad_bias = outs
+    held = [pltpu.with_memory_space_constraint(value, pltpu.VMEM) for value in (*held, consts[NAMES.index("wide")])]
+    output, grad_field, grad_spectral, grad_local, grad_bias = pl.pallas_call(
+        finish_kernel,
+        out_shape=(
+            jax.ShapeDtypeStruct(image, BF),
+            jax.ShapeDtypeStruct(image, BF),
+            jax.ShapeDtypeStruct((16, 32, 1024), F32),
+            jax.ShapeDtypeStruct((32, 32), F32),
+            jax.ShapeDtypeStruct((1, 32), F32),
+        ),
+        in_specs=[vmem] * 6,
+        out_specs=(any_spec, any_spec, any_spec, vmem, vmem),
+        scratch_shapes=[pltpu.VMEM(image, BF), dma((6,))],
+        compiler_params=pltpu.CompilerParams(vmem_limit_bytes=16 * 1024 * 1024),
+    )(*held)
     whole = (1, 1) + image
     return (
         output.reshape(whole),

time: 56.9 us -> 51.3 us (0.902)
  local copies, waits for them, and re-layouts: 5.88 us -> 0.01 us
    unnamed x13 -> x2, local copies, waits for them, and re-layouts: 5.88 us -> 0.01 us
    pallas_call x1 -> x2, Pallas kernels: 50.2 us -> 50.5 us  [the longest x1 47.8 us: local(): pl.pallas_call(functools.partial(kernel, n_slab, n_ens), out_shape=(pltpu...]
where the time goes in v3:
time: 51.3 us; the launch traced here: 51.2 us
  Pallas kernels  50.5 us (98%)
  between operations  0.66 us (1%)
    pallas_call x1, Pallas kernels, local(): pl.pallas_call(functools.partial(kernel, n_slab, n_ens), out_shape=(pltpu...  47.8 us
    pallas_call x1, Pallas kernels, local(): pl.pallas_call(finish_kernel, out_shape=(jax.ShapeDtypeStruct(image, BF),...  2.72 us

profile of v3, /device:TPU:1, one launch (start us, length us, event | category | flops | bytes accessed | tf_op | source)
XLA Modules:
  0.0 51.2 jit_solution(4020216559993837629)
XLA Ops:
  0.6 0.0 copy-start
  0.6 47.8 %shard_map.209 = (bf16[32,128,128]{2,1,0:T(8,128)(2,1)S(1)}, f32[16,32,1024]{2,1,0:T(8,128)S(1)}, f32[32,128,128]{2,1,0:T(8,128)S(1)}, bf16[4,128,256]{2,1,0:T(8,128)(2,1)S(1)}, f32[16,128]{1,0:T(8,128)S(1)}) custom-call(bf16[32,128,128]{2,1,0:T(8,128)(2,1)} %bitcast.5, bf16[16,32,1024]{2,1,0:T(8,128)(2,1)} %weight.1, bf16[32,32]{1,0:T(8,128)(2,1)} %lw.1, ...), custom_call_target="tpu_custom_call" | custom-call | tf_op jit(solution)/shard_map/pallas_call | solution.py:468
  48.5 0.0 copy-done
  48.5 2.7 %shard_map.210 = (bf16[32,128,128]{2,1,0:T(8,128)(2,1)}, bf16[32,128,128]{2,1,0:T(8,128)(2,1)}, f32[16,32,1024]{2,1,0:T(8,128)}, f32[32,32]{1,0:T(8,128)}, f32[1,32]{1,0:T(1,128)}) custom-call(bf16[32,128,128]{2,1,0:T(8,128)(2,1)S(1)} %get-tuple-element.15.out_v, f32[16,32,1024]{2,1,0:T(8,128)S(1)} %get-tuple-element.16.gs_v, ...), custom_call_target="tpu_custom_call" | custom-call | tf_op jit(solution)/shard_map/pallas_call | solution.py:515
Async XLA Ops:
  0.6 47.9 %copy-start = (bf16[256,1024]{1,0:T(8,128)(2,1)S(1)}, bf16[256,1024]{1,0:T(8,128)(2,1)}, u32[]{:S(2)}) copy-start(bf16[256,1024]{1,0:T(8,128)(2,1)} %constant.28.clone.rest_2_.wide) | copy-start | bytes 1572868

commit v4 on v3

--- a/solution.py
+++ b/solution.py
@@ -44,11 +44,14 @@
     basis = basis_table(K, N)
     slots = np.arange(NZ)
     basis_z = basis_table(K, NZ)[:, slots % 32 * 2 + slots // 32]
-    by16 = basis.astype(ml_dtypes.bfloat16).astype(np.float32)
-    wide = np.zeros((2, 8, 16, 8, N), np.float32)
-    for c in range(8):
-        wide[:, c, :, c, :] = by16.reshape(2, 16, N)
-    wide = wide.reshape(256, 8 * N)
+
+    def widen(table):
+        wide = np.zeros((2, 8, 16, 8, N), np.float32)
+        for c in range(8):
+            wide[:, c, :, c, :] = table.astype(np.float32).reshape(2, 16, N)
+        return wide.reshape(256, 8 * N)
+
+    high, low = (widen(table) for table in split_table(basis))
     eye8, eye32 = np.eye(8, dtype=np.float32), np.eye(32, dtype=np.float32)
     spread = np.repeat(np.repeat(eye8, 16, axis=0), 32, axis=1)
     to_modes = np.tile(np.repeat(eye32, 16, axis=1), (4, 1))
@@ -56,9 +59,9 @@
     rows = np.repeat(eye32, XB, axis=0)
     lanes = np.tile(rows, (1, 4))
     return dict(
-        wide_t=wide.T.copy(),
+        wide_t=high.T.copy(),
         bx=three(basis),
-        wide=wide,
+        wide=np.concatenate([high, high, low], axis=0),
         bz=three(basis_z),
         spread=np.concatenate([spread, spread], axis=0),
         to_modes=np.concatenate([to_modes, to_modes], axis=0),
@@ -68,12 +71,13 @@
         rows_t=rows.T.copy(),
         lanes=lanes,
         from_modes=np.concatenate([from_modes, from_modes], axis=1),
-        gather=np.concatenate([spread.T, spread.T], axis=0),
+        gather=spread.T.copy(),
     )
 
 
 TABLES = {name: np.asarray(table).astype(ml_dtypes.bfloat16) for name, table in tables().items()}
 NAMES = tuple(TABLES)
+WIDE = TABLES["wide"][:256]
 
 
 def split(value):
@@ -147,7 +151,8 @@
     loads[2].start()
 
     def project(data, pair):
-        return dot(jnp.concatenate(data, axis=1), tab["wide_t"][pair * 256 : (pair + 1) * 256, :])
+        tall = jnp.concatenate([jnp.concatenate(both, axis=1) for both in data], axis=0)
+        return dot(tall, tab["wide_t"][pair * 256 : (pair + 1) * 256, :])
 
     def exchange(phase):
         def one(at, carry):
@@ -218,10 +223,6 @@
         high, low = split(jnp.where(keep, tall, 0.0))
         return jnp.concatenate([high, low], axis=1)
 
-    def fold(value, keep):
-        value = jnp.where(keep, value, 0.0)
-        return value[0:32] + value[32:64] + value[64:96] + value[96:128]
-
     def to_channels(modes, keep):
         total = None
         for g in range(4):
@@ -229,17 +230,25 @@
             total = part if total is None else total + part
         return total
 
-    def weights_of(chunk, g):
-        return w_v[pl.ds(chunk * 4, 4), :, g * 256 : (g + 1) * 256].reshape(128, 256).astype(F32)
+    def own_pair_all(lanes):
+        row = lax.broadcasted_iota(jnp.int32, (512, lanes), 0) // 32
+        return row == lax.rem(lax.broadcasted_iota(jnp.int32, (512, lanes), 1), 16)
+
+    def fold_all(value, keep):
+        return jnp.sum(jnp.where(keep, value, 0.0).reshape(16, 32, value.shape[1]), axis=0)
+
+    def weights_all(g):
+        return w_v[:, :, g * 256 : (g + 1) * 256].reshape(512, 256).astype(F32)
 
     def narrow(phase, g):
         modes = jnp.concatenate([recv[phase, :32, g, :], recv[phase, 32:, g, :]], axis=1)
-        return dot_three(tab["bxt"][...], modes).astype(BF)
-
-    def put(phase, g, total):
-        modes = dot_three(tab["bx"][...], total)
-        send[phase, :32, g, :] = modes[:, :128]
-        send[phase, 32:, g, :] = modes[:, 128:]
+        return dot_three(tab["bxt"][...], modes)
+
+    def put(phase, total):
+        for g in range(4):
+            modes = dot_three(tab["bx"][...], total[g * 128 : (g + 1) * 128])
+            send[phase, :32, g, :] = modes[:, :128]
+            send[phase, 32:, g, :] = modes[:, 128:]
 
     def block_of(ref, at):
         a = ref[:, pl.ds(pl.multiple_of(at * 2 * XB, 2 * XB), XB), :].reshape(C * XB, N)
@@ -258,13 +267,11 @@
     tab_loads["wide_t"].wait()
     tab_loads["bx"].wait()
     loads[0].wait()
-    for g in range(4):
-        total = None
-        for pair in range(4):
-            at = g * 8 + pair * 2
-            part = project([field_v[at], field_v[at + 1]], pair)
-            total = part if total is None else total + part
-        put(0, g, total)
+    total = None
+    for pair in range(4):
+        part = project([[field_v[g * 8 + pair * 2 + half] for half in range(2)] for g in range(4)], pair)
+        total = part if total is None else total + part
+    put(0, total)
     pl.semaphore_wait(barrier, n_slab - 1 + n_ens - 1)
     exchange(0)
 
@@ -281,23 +288,25 @@
     kl_b[...] = jnp.where(same, tall, 0.0).astype(BF)
     pointwise(kl_f, field_v)
 
+    def add_bias(o, carry):
+        pre[o] = pre[o] + bias[o]
+        return carry
+
+    lax.fori_loop(0, C, add_bias, 0)
+
     wait_all(recv, recv_sem, 0)
     coefs = owned(0)
     call[mine] = coefs
 
-    def mix(chunk, total):
-        keep = own_pair(chunk, 128)
-        part = None
-        for g in range(4):
-            wide = dot(masked(coefs_at(call, mine, g), keep), tab["spread"][...])
-            value = wide * weights_of(chunk, g)
-            value = value[:, :128] + value[:, 128:]
-            part = value if part is None else part + value
-        high, low = split(part)
-        value = dot(jnp.concatenate([high, low], axis=1), tab["to_modes"][...])
-        return total + fold(value, own_pair(chunk, 512))
-
-    mixed = lax.fori_loop(0, 4, mix, jnp.zeros((K, 512), F32), unroll=True)
+    own, own_wide = own_pair_all(128), own_pair_all(512)
+    part = None
+    for g in range(4):
+        high, low = split(jnp.where(own, jnp.concatenate([coefs[:, g * 128 : (g + 1) * 128]] * 16, axis=0), 0.0))
+        value = dot(jnp.concatenate([high, low], axis=1), tab["spread"][...]) * weights_all(g)
+        value = value[:, :128] + value[:, 128:]
+        part = value if part is None else part + value
+    high, low = split(part)
+    mixed = fold_all(dot(jnp.concatenate([high, low], axis=1), tab["to_modes"][...]), own_wide)
     planes_out(1, mixed)
     exchange(1)
 
@@ -316,25 +325,33 @@
 
     wait_all(recv, recv_sem, 1)
     share(call.at[mine], call.at[mine], 0)
+    narrowed = []
     for g in range(4):
-        narrowed = narrow(1, g)
-        total = None
-        for pair in range(4):
-            both = dot(narrowed, tab["wide"][:, pair * 256 : (pair + 1) * 256])
-            slopes = []
+        high, low = split(narrow(1, g))
+        narrowed.append(jnp.concatenate([high, low, high], axis=1))
+    narrowed = jnp.concatenate(narrowed, axis=0)
+    total = None
+    for pair in range(4):
+        both = dot(narrowed, tab["wide"][:, pair * 256 : (pair + 1) * 256])
+        slopes = []
+        for g in range(4):
+            slopes.append([])
             for half in range(2):
                 o = g * 8 + pair * 2 + half
-                v = both[:, half * 128 : (half + 1) * 128] + (pre[o] + bias[o])
+                v = both[g * 128 : (g + 1) * 128, half * 128 : (half + 1) * 128] + pre[o]
                 cubic = (ROOT * 0.044715) * (v * v)
                 t = jnp.tanh(v * (ROOT + cubic))
                 h = 0.5 * v
-                out_v[o] = (h + h * t).astype(BF)
-                grad = (0.5 + 0.5 * t) + (h * (1.0 - t * t)) * (ROOT + 3.0 * cubic)
-                slopes.append((cot_v[o].astype(F32) * grad).astype(BF))
-                slope_v[o] = slopes[-1]
-            part = project(slopes, pair)
-            total = part if total is None else total + part
-        put(2, g, total)
+                more = 1.0 + t
+                out_v[o] = (h * more).astype(BF)
+                grad = more * (0.5 + (h * (ROOT + 3.0 * cubic)) * (1.0 - t))
+                slope = (cot_v[o].astype(F32) * grad).astype(BF)
+                slope_v[o] = slope
+                slopes[g].append(slope)
+        part = project(slopes, pair)
+        total = part if total is None else total + part
+    put(2, total)
+
     exchange(2)
 
     gacc[...] = jnp.zeros_like(gacc)
@@ -373,18 +390,15 @@
     ball[mine] = back
     share(ball.at[mine], ball.at[mine], 1)
 
-    def mix_back(chunk, total):
-        keep = own_pair(chunk, 128)
-        four = to_channels(ball[mine], keep)
-        four = jnp.concatenate([four, four], axis=1)
-        parts = []
-        for g in range(4):
-            high, low = split(weights_of(chunk, g) * four)
-            value = dot(jnp.concatenate([high, low], axis=1), tab["gather"][...])
-            parts.append(fold(value, keep))
-        return total + jnp.concatenate(parts, axis=1)
-
-    back_modes = lax.fori_loop(0, 4, mix_back, jnp.zeros((K, 512), F32), unroll=True)
+    four = None
+    for g in range(4):
+        tall = jnp.concatenate([back[:, g * 128 : (g + 1) * 128]] * 16, axis=0)
+        part = dot(jnp.where(own, tall, 0.0).astype(BF), tab["from_modes"][g, :128])
+        four = part if four is None else four + part
+    four = jnp.concatenate([four, four], axis=1)
+    tall = jnp.concatenate([(weights_all(g) * four).astype(BF) for g in range(4)], axis=0)
+    tall = dot(tall, tab["gather"][...])
+    back_modes = jnp.concatenate([fold_all(tall[g * 512 : (g + 1) * 512], own) for g in range(4)], axis=1)
     planes_out(3, back_modes)
     exchange(3)
 
@@ -413,7 +427,7 @@
 
     wait_all(recv, recv_sem, 3)
     for g in range(4):
-        s2[g] = narrow(3, g)
+        s2[g * 128 : (g + 1) * 128] = narrow(3, g).astype(BF)
     wait_sums(2, n_ens, sum_recv)
     total_out[...] = sums[2, 0] + sums[2, 1] + sums[2, 2] + sums[2, 3]
 
@@ -426,18 +440,23 @@
 
 
 def finish_kernel(out_v, gs_v, pre, s2, total, wide, out, gf, gs, gl_out, gb_out, gf_v, sems):
-    stores = [pltpu.make_async_copy(out_v, out, sems.at[4]), pltpu.make_async_copy(gs_v, gs, sems.at[5])]
+    stores = []
+    for part in range(4):
+        eight, four = pl.ds(part * 8, 8), pl.ds(part * 4, 4)
+        stores.append(pltpu.make_async_copy(gs_v.at[four], gs.at[four], sems.at[part]))
+        stores.append(pltpu.make_async_copy(out_v.at[eight], out.at[eight], sems.at[4 + part]))
     for store in stores:
         store.start()
-    for g in range(4):
-        for pair in range(4):
-            both = dot(s2[g], wide[:, pair * 256 : (pair + 1) * 256])
+    for pair in range(4):
+        both = dot(s2[...], wide[:, pair * 256 : (pair + 1) * 256])
+        for g in range(4):
+            some = pl.ds(g * 8 + pair * 2, 2)
             for half in range(2):
                 o = g * 8 + pair * 2 + half
-                gf_v[o] = (both[:, half * 128 : (half + 1) * 128] + pre[o]).astype(BF)
-        some = pl.ds(g * 8, 8)
-        stores.append(pltpu.make_async_copy(gf_v.at[some], gf.at[some], sems.at[g]))
-        stores[-1].start()
+                value = both[g * 128 : (g + 1) * 128, half * 128 : (half + 1) * 128]
+                gf_v[o] = (value + pre[o]).astype(BF)
+            stores.append(pltpu.make_async_copy(gf_v.at[some], gf.at[some], sems.at[8 + pair * 4 + g]))
+            stores[-1].start()
     for part in range(4):
         gl_out[part * 8 : (part + 1) * 8, :] = total[:8, part * 32 : (part + 1) * 32]
     gb_out[...] = total[8:9, :32]
@@ -471,7 +490,7 @@
             pltpu.VMEM(image, BF),
             pltpu.VMEM((16, 32, 1024), F32),
             pltpu.VMEM(image, F32),
-            pltpu.VMEM((4, 128, 256), BF),
+            pltpu.VMEM((512, 256), BF),
             pltpu.VMEM((16, 128), F32),
         ),
         in_specs=[any_spec, any_spec, vmem, smem, any_spec] + [any_spec] * len(NAMES),
@@ -511,7 +530,7 @@
         cotangent.reshape(image),
         *consts,
     )
-    held = [pltpu.with_memory_space_constraint(value, pltpu.VMEM) for value in (*held, consts[NAMES.index("wide")])]
+    held = [pltpu.with_memory_space_constraint(value, pltpu.VMEM) for value in (*held, jnp.asarray(WIDE))]
     output, grad_field, grad_spectral, grad_local, grad_bias = pl.pallas_call(
         finish_kernel,
         out_shape=(
@@ -523,7 +542,7 @@
         ),
         in_specs=[vmem] * 6,
         out_specs=(any_spec, any_spec, any_spec, vmem, vmem),
-        scratch_shapes=[pltpu.VMEM(image, BF), dma((6,))],
+        scratch_shapes=[pltpu.VMEM(image, BF), dma((24,))],
         compiler_params=pltpu.CompilerParams(vmem_limit_bytes=16 * 1024 * 1024),
     )(*held)
     whole = (1, 1) + image

time: 51.3 us -> 50.5 us (0.984)
  Pallas kernels: 50.5 us -> 49.8 us
    pallas_call x1, Pallas kernels: 47.8 us -> 46.9 us  [local(): pl.pallas_call(functools.partial(kernel, n_slab, n_ens), out_shape=(pltpu...]
where the time goes in v4:
time: 50.5 us; the launch traced here: 50.4 us
  Pallas kernels  49.8 us (99%)
  between operations  0.66 us (1%)
    pallas_call x1, Pallas kernels, local(): pl.pallas_call(functools.partial(kernel, n_slab, n_ens), out_shape=(pltpu...  46.9 us
    pallas_call x1, Pallas kernels, local(): pl.pallas_call(finish_kernel, out_shape=(jax.ShapeDtypeStruct(image, BF),...  2.84 us

profile of v4, /device:TPU:1, one launch (start us, length us, event | category | flops | bytes accessed | tf_op | source)
XLA Modules:
  0.0 50.4 jit_solution(17142840477351835933)
XLA Ops:
  0.6 0.0 copy-start
  0.6 46.9 %shard_map.218 = (bf16[32,128,128]{2,1,0:T(8,128)(2,1)S(1)}, f32[16,32,1024]{2,1,0:T(8,128)S(1)}, f32[32,128,128]{2,1,0:T(8,128)S(1)}, bf16[512,256]{1,0:T(8,128)(2,1)S(1)}, f32[16,128]{1,0:T(8,128)S(1)}) custom-call(bf16[32,128,128]{2,1,0:T(8,128)(2,1)} %bitcast.5, bf16[16,32,1024]{2,1,0:T(8,128)(2,1)} %weight.1, bf16[32,32]{1,0:T(8,128)(2,1)} %lw.1, ...), custom_call_target="tpu_custom_call" | custom-call | tf_op jit(solution)/shard_map/pallas_call | solution.py:487
  47.6 0.0 copy-done
  47.6 2.8 %shard_map.219 = (bf16[32,128,128]{2,1,0:T(8,128)(2,1)}, bf16[32,128,128]{2,1,0:T(8,128)(2,1)}, f32[16,32,1024]{2,1,0:T(8,128)}, f32[32,32]{1,0:T(8,128)}, f32[1,32]{1,0:T(1,128)}) custom-call(bf16[32,128,128]{2,1,0:T(8,128)(2,1)S(1)} %get-tuple-element.15.out_v, f32[16,32,1024]{2,1,0:T(8,128)S(1)} %get-tuple-element.16.gs_v, ...), custom_call_target="tpu_custom_call" | custom-call | tf_op jit(solution)/shard_map/pallas_call | solution.py:534
Async XLA Ops:
  0.6 47.0 %copy-start = (bf16[256,1024]{1,0:T(8,128)(2,1)S(1)}, bf16[256,1024]{1,0:T(8,128)(2,1)}, u32[]{:S(2)}) copy-start(bf16[256,1024]{1,0:T(8,128)(2,1)} %constant.41.clone.wide) | copy-start | bytes 1572868

commit v5 on v4

--- a/solution.py
+++ b/solution.py
@@ -102,13 +102,7 @@
     return size // 2 + (at + 1) // 2 * (2 * lax.rem(at + 1, 2) - 1)
 
 
-def far_first(me, at):
-    x = lax.rem(me // 16 + middle_out(lax.rem(at // 2, 4), 4), 4)
-    z = lax.rem(lax.rem(me // 2, 8) + middle_out(at // 8, 8), 8)
-    return x * 16 + z * 2 + lax.rem(me + 1 + at, 2)
-
-
-def kernel(n_slab, n_ens, field, weight, lw, bias, cot, *rest):
+def kernel(n_slab, n_ens, field, weight, lw_in, bias_in, cot, *rest):
     consts = dict(zip(NAMES, rest[: len(NAMES)]))
     rest = rest[len(NAMES) :]
     out_v, gs_v, pre, s2, total_out = rest[:5]
@@ -116,13 +110,15 @@
     tab = dict(zip(NAMES, rest[: len(NAMES)]))
     rest = rest[len(NAMES) :]
     (
-        field_v, cot_v, w_v, slope_v, kl_f, kl_b, cexp, gacc,
+        field_v, cot_v, w_v, lw, bias, slope_v, kl_f, kl_b, cexp, gacc,
         send, recv, call, ball, sums,
         load_sem, tab_sem, send_sem, recv_sem, ens_send, ens_recv, sum_send, sum_recv,
     ) = rest
     me = lax.axis_index("slab")
     mine = lax.axis_index("ens")
     x, z, core = me // 16, lax.rem(me // 2, 8), lax.rem(me, 2)
+    my_slot = core * 32 + me // 2
+    places = [(lax.rem(x + at, 4), lax.rem(core + 1 + other, 2)) for at in (2, 1, 3, 0) for other in range(2)]
 
     barrier = pltpu.get_barrier_semaphore()
 
@@ -138,6 +134,8 @@
         pltpu.make_async_copy(field, field_v, load_sem.at[0]),
         pltpu.make_async_copy(cot, cot_v, load_sem.at[1]),
         pltpu.make_async_copy(weight, w_v, load_sem.at[2]),
+        pltpu.make_async_copy(lw_in, lw, load_sem.at[3]),
+        pltpu.make_async_copy(bias_in, bias, load_sem.at[4]),
     ]
     tab_loads = {
         name: pltpu.make_async_copy(consts[name], tab[name], tab_sem.at[at])
@@ -147,28 +145,34 @@
     loads[0].start()
     for name in NAMES[1:]:
         tab_loads[name].start()
-    loads[1].start()
-    loads[2].start()
+    for load in loads[1:]:
+        load.start()
 
     def project(data, pair):
         tall = jnp.concatenate([jnp.concatenate(both, axis=1) for both in data], axis=0)
         return dot(tall, tab["wide_t"][pair * 256 : (pair + 1) * 256, :])
 
     def exchange(phase):
-        def one(at, carry):
-            peer = far_first(me, at)
+        def one(to_x, to_z, to_core):
             pltpu.make_async_remote_copy(
-                src_ref=send.at[phase, slot(peer)],
-                dst_ref=recv.at[phase, slot(me)],
+                src_ref=send.at[phase, to_core * 32 + to_x * 8 + to_z],
+                dst_ref=recv.at[phase, my_slot],
                 send_sem=send_sem.at[phase],
                 recv_sem=recv_sem.at[phase],
-                device_id={"slab": peer},
+                device_id={"slab": to_x * 16 + to_z * 2 + to_core},
                 device_id_type=MESH,
             ).start()
+
+        def ring(at, carry):
+            to_z = lax.rem(z + middle_out(at, 8), 8)
+            for to_x, to_core in places:
+                one(to_x, to_z, to_core)
             return carry
 
-        lax.fori_loop(0, n_slab - 1, one, 0)
-        recv[phase, slot(me)] = send[phase, slot(me)]
+        lax.fori_loop(0, 7, ring, 0)
+        for to_x, to_core in places[:-1]:
+            one(to_x, z, to_core)
+        recv[phase, my_slot] = send[phase, my_slot]
 
     def share(source, target, at_sem):
         for at in range(1, n_ens):
@@ -277,8 +281,8 @@
 
     for name in NAMES[2:]:
         tab_loads[name].wait()
-    loads[1].wait()
-    loads[2].wait()
+    for load in loads[1:]:
+        load.wait()
     tall = dot(dot_nt(tab["rows"][...], lw[...]).astype(BF), tab["rows_t"][...])
     same = lax.rem(lax.broadcasted_iota(jnp.int32, (512, 512), 0), XB) == lax.rem(
         lax.broadcasted_iota(jnp.int32, (512, 512), 1), XB
@@ -439,12 +443,17 @@
     wait_share_sent(ball, 1)
 
 
-def finish_kernel(out_v, gs_v, pre, s2, total, wide, out, gf, gs, gl_out, gb_out, gf_v, sems):
+def finish_kernel(out_v, gs_v, pre, s2, total, wide, out, gf, gs, gl, gb, gf_v, gl_v, gb_v, sems):
     stores = []
     for part in range(4):
         eight, four = pl.ds(part * 8, 8), pl.ds(part * 4, 4)
         stores.append(pltpu.make_async_copy(gs_v.at[four], gs.at[four], sems.at[part]))
         stores.append(pltpu.make_async_copy(out_v.at[eight], out.at[eight], sems.at[4 + part]))
+    for part in range(4):
+        gl_v[part * 8 : (part + 1) * 8, :] = total[:8, part * 32 : (part + 1) * 32]
+    gb_v[...] = total[8:9, :32]
+    stores.append(pltpu.make_async_copy(gl_v, gl, sems.at[24]))
+    stores.append(pltpu.make_async_copy(gb_v, gb, sems.at[25]))
     for store in stores:
         store.start()
     for pair in range(4):
@@ -457,15 +466,8 @@
                 gf_v[o] = (value + pre[o]).astype(BF)
             stores.append(pltpu.make_async_copy(gf_v.at[some], gf.at[some], sems.at[8 + pair * 4 + g]))
             stores[-1].start()
-    for part in range(4):
-        gl_out[part * 8 : (part + 1) * 8, :] = total[:8, part * 32 : (part + 1) * 32]
-    gb_out[...] = total[8:9, :32]
     for store in stores:
         store.wait()
-
-
-def slot(device):
-    return lax.rem(device, 2) * 32 + device // 2
 
 
 def coefs_at(ref, member, g):
@@ -481,7 +483,6 @@
     consts = [jnp.asarray(TABLES[name]) for name in NAMES]
     any_spec = pl.BlockSpec(memory_space=pl.ANY)
     vmem = pl.BlockSpec(memory_space=pltpu.VMEM)
-    smem = pl.BlockSpec(memory_space=pltpu.SMEM)
     image = (C, N, N)
     dma = pltpu.SemaphoreType.DMA
     held = pl.pallas_call(
@@ -493,13 +494,15 @@
             pltpu.VMEM((512, 256), BF),
             pltpu.VMEM((16, 128), F32),
         ),
-        in_specs=[any_spec, any_spec, vmem, smem, any_spec] + [any_spec] * len(NAMES),
+        in_specs=[any_spec] * 5 + [any_spec] * len(NAMES),
         out_specs=(vmem,) * 5,
         scratch_shapes=[pltpu.VMEM(TABLES[name].shape, BF) for name in NAMES]
         + [
             pltpu.VMEM(image, BF),
             pltpu.VMEM(image, BF),
             pltpu.VMEM((16, 32, 1024), BF),
+            pltpu.VMEM((32, 32), BF),
+            pltpu.SMEM((32,), F32),
             pltpu.VMEM(image, BF),
             pltpu.VMEM((512, 512), BF),
             pltpu.VMEM((512, 512), BF),
@@ -510,7 +513,7 @@
             pltpu.VMEM((n_ens, K, 512), F32),
             pltpu.VMEM((n_ens, K, 512), F32),
             pltpu.VMEM((3, 8, 16, 128), F32),
-            dma((3,)),
+            dma((5,)),
             dma((len(NAMES),)),
             dma((4,)),
             dma((4,)),
@@ -541,8 +544,8 @@
             jax.ShapeDtypeStruct((1, 32), F32),
         ),
         in_specs=[vmem] * 6,
-        out_specs=(any_spec, any_spec, any_spec, vmem, vmem),
-        scratch_shapes=[pltpu.VMEM(image, BF), dma((24,))],
+        out_specs=(any_spec,) * 5,
+        scratch_shapes=[pltpu.VMEM(image, BF), pltpu.VMEM((32, 32), F32), pltpu.VMEM((1, 32), F32), dma((26,))],
         compiler_params=pltpu.CompilerParams(vmem_limit_bytes=16 * 1024 * 1024),
     )(*held)
     whole = (1, 1) + image

time: 50.5 us -> 46.4 us (0.919)
  Pallas kernels: 49.8 us -> 45.6 us
    pallas_call x1, Pallas kernels: 46.9 us -> 43.4 us  [local(): pl.pallas_call(functools.partial(kernel, n_slab, n_ens), out_shape=(pltpu...]
    pallas_call x1, Pallas kernels: 2.84 us -> 2.22 us  [local(): pl.pallas_call(finish_kernel, out_shape=(jax.ShapeDtypeStruct(image, BF),...]
where the time goes in v5:
time: 46.4 us; the launch traced here: 46.3 us
  Pallas kernels  45.6 us (98%)
  between operations  0.66 us (1%)
    pallas_call x1, Pallas kernels, local(): pl.pallas_call(functools.partial(kernel, n_slab, n_ens), out_shape=(pltpu...  43.4 us
    pallas_call x1, Pallas kernels, local(): pl.pallas_call(finish_kernel, out_shape=(jax.ShapeDtypeStruct(image, BF),...  2.22 us

profile of v5, /device:TPU:1, one launch (start us, length us, event | category | flops | bytes accessed | tf_op | source)
XLA Modules:
  0.0 46.3 jit_solution(17824886391714267516)
XLA Ops:
  0.6 0.0 copy-start
  0.6 43.4 %shard_map.218 = (bf16[32,128,128]{2,1,0:T(8,128)(2,1)S(1)}, f32[16,32,1024]{2,1,0:T(8,128)S(1)}, f32[32,128,128]{2,1,0:T(8,128)S(1)}, bf16[512,256]{1,0:T(8,128)(2,1)S(1)}, f32[16,128]{1,0:T(8,128)S(1)}) custom-call(bf16[32,128,128]{2,1,0:T(8,128)(2,1)} %bitcast.5, bf16[16,32,1024]{2,1,0:T(8,128)(2,1)} %weight.1, bf16[32,32]{1,0:T(8,128)(2,1)} %lw_in.1, ...), custom_call_target="tpu_custom_call" | custom-call | tf_op jit(solution)/shard_map/pallas_call | solution.py:488
  44.1 0.0 copy-done
  44.1 2.2 %shard_map.219 = (bf16[32,128,128]{2,1,0:T(8,128)(2,1)}, bf16[32,128,128]{2,1,0:T(8,128)(2,1)}, f32[16,32,1024]{2,1,0:T(8,128)}, f32[32,32]{1,0:T(8,128)}, f32[1,32]{1,0:T(1,128)}) custom-call(bf16[32,128,128]{2,1,0:T(8,128)(2,1)S(1)} %get-tuple-element.15.out_v, f32[16,32,1024]{2,1,0:T(8,128)S(1)} %get-tuple-element.16.gs_v, ...), custom_call_target="tpu_custom_call" | custom-call | tf_op jit(solution)/shard_map/pallas_call | solution.py:537
Async XLA Ops:
  0.6 43.4 %copy-start = (bf16[256,1024]{1,0:T(8,128)(2,1)S(1)}, bf16[256,1024]{1,0:T(8,128)(2,1)}, u32[]{:S(2)}) copy-start(bf16[256,1024]{1,0:T(8,128)(2,1)} %constant.41.clone.wide) | copy-start | bytes 1572868

commit v6 on v5

--- a/solution.py
+++ b/solution.py
@@ -126,7 +126,7 @@
         pl.semaphore_signal(barrier, inc=1, device_id={"slab": lax.rem(me + at, n_slab)}, device_id_type=MESH)
         return carry
 
-    lax.fori_loop(1, n_slab, greet, 0)
+    lax.fori_loop(1, n_slab, greet, 0, unroll=21)
     for at in range(1, n_ens):
         pl.semaphore_signal(barrier, inc=1, device_id={"ens": lax.rem(mine + at, n_ens)}, device_id_type=MESH)
 
@@ -169,7 +169,16 @@
                 one(to_x, to_z, to_core)
             return carry
 
-        lax.fori_loop(0, 7, ring, 0)
+        def both(at, carry):
+            for to in (4 - at, 4 + at):
+                to_z = lax.rem(z + to, 8)
+                for to_x, to_core in places:
+                    one(to_x, to_z, to_core)
+            return carry
+
+        for to_x, to_core in places:
+            one(to_x, lax.rem(z + 4, 8), to_core)
+        lax.fori_loop(1, 4, both, 0)
         for to_x, to_core in places[:-1]:
             one(to_x, z, to_core)
         recv[phase, my_slot] = send[phase, my_slot]

time: 46.4 us -> 45.8 us (0.987)
  Pallas kernels: 45.6 us -> 45 us
    pallas_call x1, Pallas kernels: 43.4 us -> 42.8 us  [local(): pl.pallas_call(functools.partial(kernel, n_slab, n_ens), out_shape=(pltpu...]
where the time goes in v6:
time: 45.8 us; the launch traced here: 45.7 us
  Pallas kernels  45 us (98%)
  between operations  0.66 us (1%)
    pallas_call x1, Pallas kernels, local(): pl.pallas_call(functools.partial(kernel, n_slab, n_ens), out_shape=(pltpu...  42.8 us
    pallas_call x1, Pallas kernels, local(): pl.pallas_call(finish_kernel, out_shape=(jax.ShapeDtypeStruct(image, BF),...  2.22 us

profile of v6, /device:TPU:1, one launch (start us, length us, event | category | flops | bytes accessed | tf_op | source)
XLA Modules:
  0.0 45.7 jit_solution(992520768228314216)
XLA Ops:
  0.6 0.0 copy-start
  0.6 42.8 %shard_map.218 = (bf16[32,128,128]{2,1,0:T(8,128)(2,1)S(1)}, f32[16,32,1024]{2,1,0:T(8,128)S(1)}, f32[32,128,128]{2,1,0:T(8,128)S(1)}, bf16[512,256]{1,0:T(8,128)(2,1)S(1)}, f32[16,128]{1,0:T(8,128)S(1)}) custom-call(bf16[32,128,128]{2,1,0:T(8,128)(2,1)} %bitcast.5, bf16[16,32,1024]{2,1,0:T(8,128)(2,1)} %weight.1, bf16[32,32]{1,0:T(8,128)(2,1)} %lw_in.1, ...), custom_call_target="tpu_custom_call" | custom-call | tf_op jit(solution)/shard_map/pallas_call | solution.py:497
  43.4 0.0 copy-done
  43.4 2.2 %shard_map.219 = (bf16[32,128,128]{2,1,0:T(8,128)(2,1)}, bf16[32,128,128]{2,1,0:T(8,128)(2,1)}, f32[16,32,1024]{2,1,0:T(8,128)}, f32[32,32]{1,0:T(8,128)}, f32[1,32]{1,0:T(1,128)}) custom-call(bf16[32,128,128]{2,1,0:T(8,128)(2,1)S(1)} %get-tuple-element.15.out_v, f32[16,32,1024]{2,1,0:T(8,128)S(1)} %get-tuple-element.16.gs_v, ...), custom_call_target="tpu_custom_call" | custom-call | tf_op jit(solution)/shard_map/pallas_call | solution.py:546
Async XLA Ops:
  0.6 42.8 %copy-start = (bf16[256,1024]{1,0:T(8,128)(2,1)S(1)}, bf16[256,1024]{1,0:T(8,128)(2,1)}, u32[]{:S(2)}) copy-start(bf16[256,1024]{1,0:T(8,128)(2,1)} %constant.41.clone.wide) | copy-start | bytes 1572868

commit v7 on v6

--- a/solution.py
+++ b/solution.py
@@ -244,8 +244,9 @@
         return total
 
     def own_pair_all(lanes):
-        row = lax.broadcasted_iota(jnp.int32, (512, lanes), 0) // 32
-        return row == lax.rem(lax.broadcasted_iota(jnp.int32, (512, lanes), 1), 16)
+        lane = lax.rem(lax.broadcasted_iota(jnp.int32, (32, lanes), 1), 16)
+        row = jnp.concatenate([jnp.full((32, lanes), j, jnp.int32) for j in range(16)], axis=0)
+        return row == jnp.concatenate([lane] * 16, axis=0)
 
     def fold_all(value, keep):
         return jnp.sum(jnp.where(keep, value, 0.0).reshape(16, 32, value.shape[1]), axis=0)

time: 45.8 us -> 45.7 us (level)
  no operation moved by 1% of the time
where the time goes in v7:
time: 45.7 us; the launch traced here: 45.6 us
  Pallas kernels  45 us (98%)
  between operations  0.66 us (1%)
    pallas_call x1, Pallas kernels, local(): pl.pallas_call(functools.partial(kernel, n_slab, n_ens), out_shape=(pltpu...  42.8 us
    pallas_call x1, Pallas kernels, local(): pl.pallas_call(finish_kernel, out_shape=(jax.ShapeDtypeStruct(image, BF),...  2.22 us

profile of v7, /device:TPU:1, one launch (start us, length us, event | category | flops | bytes accessed | tf_op | source)
XLA Modules:
  0.0 45.6 jit_solution(9680500534083153940)
XLA Ops:
  0.6 0.0 copy-start
  0.6 42.8 %shard_map.218 = (bf16[32,128,128]{2,1,0:T(8,128)(2,1)S(1)}, f32[16,32,1024]{2,1,0:T(8,128)S(1)}, f32[32,128,128]{2,1,0:T(8,128)S(1)}, bf16[512,256]{1,0:T(8,128)(2,1)S(1)}, f32[16,128]{1,0:T(8,128)S(1)}) custom-call(bf16[32,128,128]{2,1,0:T(8,128)(2,1)} %bitcast.5, bf16[16,32,1024]{2,1,0:T(8,128)(2,1)} %weight.1, bf16[32,32]{1,0:T(8,128)(2,1)} %lw_in.1, ...), custom_call_target="tpu_custom_call" | custom-call | tf_op jit(solution)/shard_map/pallas_call | solution.py:498
  43.4 0.0 copy-done
  43.4 2.2 %shard_map.219 = (bf16[32,128,128]{2,1,0:T(8,128)(2,1)}, bf16[32,128,128]{2,1,0:T(8,128)(2,1)}, f32[16,32,1024]{2,1,0:T(8,128)}, f32[32,32]{1,0:T(8,128)}, f32[1,32]{1,0:T(1,128)}) custom-call(bf16[32,128,128]{2,1,0:T(8,128)(2,1)S(1)} %get-tuple-element.15.out_v, f32[16,32,1024]{2,1,0:T(8,128)S(1)} %get-tuple-element.16.gs_v, ...), custom_call_target="tpu_custom_call" | custom-call | tf_op jit(solution)/shard_map/pallas_call | solution.py:547
Async XLA Ops:
  0.6 42.8 %copy-start = (bf16[256,1024]{1,0:T(8,128)(2,1)S(1)}, bf16[256,1024]{1,0:T(8,128)(2,1)}, u32[]{:S(2)}) copy-start(bf16[256,1024]{1,0:T(8,128)(2,1)} %constant.41.clone.wide) | copy-start | bytes 1572868
